TPU v7x, 32 devices: a whole 2x2x4 slice. The times are simulated.
32 devices in a mesh: row: 8 (over z, x), pair: 4 (over y, core).
Axes of the slice: x: 2, y: 2, z: 4, core: 2. Of those that a mesh axis runs over, the one named last changes fastest.
Arguments:
- snapshots: float32 [4096, 2048], P('row', 'pair'), may hold values from -16 to 16
- pairing: int32 [2, 16], replicated, may hold values from 0 to 15, as said below
Outputs:
- left_vectors: float32 [4096, 2048], P('row', 'pair')
- spectrum: float32 [2048], P('pair')
Inputs may be any that keep to these rules, and one draw needn't show every extreme that they name: Each row of pairing is a permutation of 0 to 15; slots 2k and 2k + 1 of a row form a pair; no two blocks are paired in more than one round.
All inputs are finite; a program needn't handle non-finite values.
Results may differ from a plain program's by a relative error of at most 0.0003.
Values sent between devices are 32-bit elements; how exact they have to be, the bound alone decides.
No kernel may reach another device: no remote copies, remote signals or barrier semaphores. Data moves between devices by JAX's collectives and lax.ppermute only.
A program may use at most 64 MiB of HBM per device.

v0:
```python
import jax
import jax.numpy as jnp
from jax import lax
from jax.sharding import PartitionSpec as P

BLOCK = 128
ROUNDS = 2
EIG_ITERS = 3


precise = lax.Precision.HIGHEST
epsilon = 1e-06


def orthogonal_factor(gram_pair):
    order_size = gram_pair.shape[-1]
    rotation = jnp.broadcast_to(jnp.eye(order_size, dtype=jnp.float32), gram_pair.shape)
    for iteration in range(EIG_ITERS):
        image = jnp.matmul(gram_pair, rotation, precision=precise)
        inner = jnp.matmul(jnp.swapaxes(image, -1, -2), image, precision=precise)
        factor_lower = jnp.linalg.cholesky(inner)
        solved = jax.scipy.linalg.solve_triangular(
            factor_lower, jnp.swapaxes(image, -1, -2), lower=True
        )
        rotation = jnp.swapaxes(solved, -1, -2)
    return rotation


def selector(current, target, slots_dev, first_slot):
    wanted = lax.dynamic_slice_in_dim(target, first_slot, slots_dev)
    return (current[:, None] == wanted[None, :]).astype(jnp.float32)


def placing(selection):

    def folding(carried, pieces, offset):
        return tuple(
            (jnp.einsum("rnc,nk->rkc", segment, selection, precision=precise) for segment in pieces)
        )

    return folding


def whole_gram(paired):
    partial_gram = jnp.einsum("rpi,rpj->pij", paired, paired, precision=precise)
    return lax.psum(partial_gram, "row")


def shards(snapshots, pairing):
    rows_dev = snapshots.shape[0]
    slots_dev = snapshots.shape[1] // BLOCK
    total_blocks = pairing.shape[1]
    first_slot = lax.axis_index("pair") * slots_dev
    blocks = snapshots.reshape(rows_dev, slots_dev, BLOCK)
    current = jnp.arange(total_blocks, dtype=jnp.int32)
    target = pairing[0]
    folding = placing(selector(current, target, slots_dev, first_slot))
    (blocks,) = folding(
        (jnp.zeros_like(blocks),),
        (lax.all_gather(blocks, "pair", axis=1, tiled=True),),
        jnp.int32(0),
    )
    for sweep_index in range(ROUNDS):
        if sweep_index > 0:
            target = pairing[sweep_index]
            folding = placing(selector(current, target, slots_dev, first_slot))
            (blocks,) = folding(
                (jnp.zeros_like(blocks),),
                (lax.all_gather(blocks, "pair", axis=1, tiled=True),),
                jnp.int32(0),
            )
        current = target
        paired = blocks.reshape(rows_dev, slots_dev // 2, 2 * BLOCK)
        gram_pair = whole_gram(paired)
        rotation = orthogonal_factor(gram_pair)
        rotated = jnp.einsum("rpi,pij->rpj", paired, rotation, precision=precise)
        blocks = rotated.reshape(rows_dev, slots_dev, BLOCK)
    target = jnp.arange(total_blocks, dtype=jnp.int32)
    folding = placing(selector(current, target, slots_dev, first_slot))
    (blocks,) = folding(
        (jnp.zeros_like(blocks),),
        (lax.all_gather(blocks, "pair", axis=1, tiled=True),),
        jnp.int32(0),
    )
    squares = lax.psum(jnp.sum(blocks * blocks, axis=0), "row")
    total_rows = rows_dev * lax.axis_size("row")
    spectrum = jnp.sqrt(squares / total_rows + epsilon)
    left_vectors = blocks / spectrum[None]
    return (left_vectors.reshape(rows_dev, slots_dev * BLOCK), spectrum.reshape(slots_dev * BLOCK))


def solution(mesh):
    return jax.shard_map(
        shards,
        mesh=mesh,
        in_specs=(P("row", "pair"), P()),
        out_specs=(P("row", "pair"), P("pair")),
        check_vma=False,
    )
```

profile of v0, /device:TPU:0, one launch (start us, length us, event | category | flops | bytes accessed | tf_op | source)
XLA Modules:
  0.0 1024.0 jit_solution(16187612288344215851)
XLA Ops:
  10.3 37.2 %all-gather.4.cloned.1.call-done = f32[512,16,128]{2,0,1:T(8,128)} async-done(((f32[512,4,128]{2,0,1:T(8,128)}), f32[512,16,128]{2,0,1:T(8,128)}) %all-gather.4.cloned.1.call-update) | async-done | bytes 4194320 | tf_op jit(solution)/shard_map/all_gather | solution.py:60
  57.2 72.4 %all-reduce.4.cloned.1.call-done = f32[2,256,256]{2,1,0:T(8,128)} async-done(((f32[2,256,256]{2,1,0:T(8,128)}), f32[2,256,256]{2,1,0:T(8,128)}) %all-reduce.4.cloned.1.call-update) | async-done | bytes 524304 | tf_op jit(solution)/shard_map/psum | solution.py:46
  133.4 23.9 %custom-call.33 = f32[2,128,128]{2,1,0:T(8,128)S(1)} custom-call(f32[2,128,128]{2,1,0:T(8,128)S(1)} %cholesky.502), custom_call_target="Cholesky" | custom-call | tf_op jit(solution)/shard_map/jit(cholesky)/cholesky | solution.py:21
  179.6 23.5 %custom-call.35 = f32[2,128,128]{2,1,0:T(8,128)S(1)} custom-call(f32[2,128,128]{2,1,0:T(8,128)S(1)} %convolution_subtract_fusion.11), custom_call_target="Cholesky" | custom-call | tf_op jit(solution)/shard_map/jit(cholesky)/cholesky | solution.py:21
  207.7 39.5 %custom-call.36 = f32[2,2,128,128]{2,3,1,0:T(8,128)S(1)} custom-call(f32[2,2,128,128]{3,2,1,0:T(8,128)S(1)} %bitcast.299), custom_call_target="InvertDiagBlocksLowerTriangular" | custom-call | tf_op jit(solution)/shard_map/jit(_solve_triangular)/vmap()/triangular_solve | solution.py:22
  251.5 23.5 %custom-call.37 = f32[2,128,128]{2,1,0:T(8,128)S(1)} custom-call(f32[2,128,128]{2,1,0:T(8,128)S(1)} %cholesky.505), custom_call_target="Cholesky" | custom-call | tf_op jit(solution)/shard_map/jit(cholesky)/cholesky | solution.py:21
  297.2 23.7 %custom-call.39 = f32[2,128,128]{2,1,0:T(8,128)S(1)} custom-call(f32[2,128,128]{2,1,0:T(8,128)S(1)} %convolution_subtract_fusion.10), custom_call_target="Cholesky" | custom-call | tf_op jit(solution)/shard_map/jit(cholesky)/cholesky | solution.py:21
  325.4 39.3 %custom-call.40 = f32[2,2,128,128]{2,3,1,0:T(8,128)S(1)} custom-call(f32[2,2,128,128]{3,2,1,0:T(8,128)S(1)} %bitcast.300), custom_call_target="InvertDiagBlocksLowerTriangular" | custom-call | tf_op jit(solution)/shard_map/jit(_solve_triangular)/vmap()/triangular_solve | solution.py:22
  368.3 23.9 %custom-call.41 = f32[2,128,128]{2,1,0:T(8,128)S(1)} custom-call(f32[2,128,128]{2,1,0:T(8,128)S(1)} %cholesky.508), custom_call_target="Cholesky" | custom-call | tf_op jit(solution)/shard_map/jit(cholesky)/cholesky | solution.py:21
  412.5 23.5 %custom-call.43 = f32[2,128,128]{2,1,0:T(8,128)S(1)} custom-call(f32[2,128,128]{2,1,0:T(8,128)S(1)} %convolution_subtract_fusion.9), custom_call_target="Cholesky" | custom-call | tf_op jit(solution)/shard_map/jit(cholesky)/cholesky | solution.py:21
  440.6 39.5 %custom-call.44 = f32[2,2,128,128]{2,3,1,0:T(8,128)S(1)} custom-call(f32[2,2,128,128]{3,2,1,0:T(8,128)S(1)} %bitcast.301), custom_call_target="InvertDiagBlocksLowerTriangular" | custom-call | tf_op jit(solution)/shard_map/jit(_solve_triangular)/vmap()/triangular_solve | solution.py:22
  484.1 33.8 %all-gather.6.cloned.1.call-done = f32[512,16,128]{2,0,1:T(8,128)} async-done(((f32[512,4,128]{2,0,1:T(8,128)}), f32[512,16,128]{2,0,1:T(8,128)}) %all-gather.6.cloned.1.call-update) | async-done | bytes 4194320 | tf_op jit(solution)/shard_map/all_gather | solution.py:69
  527.6 72.3 %all-reduce.6.cloned.1.call-done = f32[2,256,256]{2,1,0:T(8,128)} async-done(((f32[2,256,256]{2,1,0:T(8,128)}), f32[2,256,256]{2,1,0:T(8,128)}) %all-reduce.6.cloned.1.call-update) | async-done | bytes 524304 | tf_op jit(solution)/shard_map/psum | solution.py:46
  603.7 23.5 %custom-call.45 = f32[2,128,128]{2,1,0:T(8,128)S(1)} custom-call(f32[2,128,128]{2,1,0:T(8,128)S(1)} %cholesky.511), custom_call_target="Cholesky" | custom-call | tf_op jit(solution)/shard_map/jit(cholesky)/cholesky | solution.py:21
  649.4 23.5 %custom-call.47 = f32[2,128,128]{2,1,0:T(8,128)S(1)} custom-call(f32[2,128,128]{2,1,0:T(8,128)S(1)} %convolution_subtract_fusion.8), custom_call_target="Cholesky" | custom-call | tf_op jit(solution)/shard_map/jit(cholesky)/cholesky | solution.py:21
  677.4 39.7 %custom-call.48 = f32[2,2,128,128]{2,3,1,0:T(8,128)S(1)} custom-call(f32[2,2,128,128]{3,2,1,0:T(8,128)S(1)} %bitcast.302), custom_call_target="InvertDiagBlocksLowerTriangular" | custom-call | tf_op jit(solution)/shard_map/jit(_solve_triangular)/vmap()/triangular_solve | solution.py:22
  721.4 23.5 %custom-call.49 = f32[2,128,128]{2,1,0:T(8,128)S(1)} custom-call(f32[2,128,128]{2,1,0:T(8,128)S(1)} %cholesky.514), custom_call_target="Cholesky" | custom-call | tf_op jit(solution)/shard_map/jit(cholesky)/cholesky | solution.py:21
  767.1 23.6 %custom-call.51 = f32[2,128,128]{2,1,0:T(8,128)S(1)} custom-call(f32[2,128,128]{2,1,0:T(8,128)S(1)} %convolution_subtract_fusion.7), custom_call_target="Cholesky" | custom-call | tf_op jit(solution)/shard_map/jit(cholesky)/cholesky | solution.py:21
  795.3 39.3 %custom-call.52 = f32[2,2,128,128]{2,3,1,0:T(8,128)S(1)} custom-call(f32[2,2,128,128]{3,2,1,0:T(8,128)S(1)} %bitcast.303), custom_call_target="InvertDiagBlocksLowerTriangular" | custom-call | tf_op jit(solution)/shard_map/jit(_solve_triangular)/vmap()/triangular_solve | solution.py:22
  838.1 23.7 %custom-call.53 = f32[2,128,128]{2,1,0:T(8,128)S(1)} custom-call(f32[2,128,128]{2,1,0:T(8,128)S(1)} %cholesky.517), custom_call_target="Cholesky" | custom-call | tf_op jit(solution)/shard_map/jit(cholesky)/cholesky | solution.py:21
  882.2 23.5 %custom-call.55 = f32[2,128,128]{2,1,0:T(8,128)S(1)} custom-call(f32[2,128,128]{2,1,0:T(8,128)S(1)} %convolution_subtract_fusion.6), custom_call_target="Cholesky" | custom-call | tf_op jit(solution)/shard_map/jit(cholesky)/cholesky | solution.py:21
  910.3 39.6 %custom-call.56 = f32[2,2,128,128]{2,3,1,0:T(8,128)S(1)} custom-call(f32[2,2,128,128]{3,2,1,0:T(8,128)S(1)} %bitcast.298), custom_call_target="InvertDiagBlocksLowerTriangular" | custom-call | tf_op jit(solution)/shard_map/jit(_solve_triangular)/vmap()/triangular_solve | solution.py:22
  953.8 33.8 %all-gather.8.cloned.1.call-done = f32[512,16,128]{2,0,1:T(8,128)} async-done(((f32[512,4,128]{2,0,1:T(8,128)}), f32[512,16,128]{2,0,1:T(8,128)}) %all-gather.8.cloned.1.call-update) | async-done | bytes 4194320 | tf_op jit(solution)/shard_map/all_gather | solution.py:82
  993.9 21.4 %psum.23 = f32[4,128]{1,0:T(4,128)S(1)} all-reduce(f32[4,128]{1,0:T(4,128)S(1)} %get-tuple-element.144), channel_id=1, replica_groups=mesh['row'=8,'pair'=4] {'row'}, use_global_device_ids=true, to_apply=%region_7.10 | all-reduce | flops 512 | bytes 4096 | tf_op jit(solution)/shard_map/psum | solution.py:85
  (207 shorter events, 242.5 us)
Async XLA Ops:
  7.2 3.0 copy-start.6
  7.2 40.3 %all-gather.4.cloned.1.call-start = ((), (), s32[]{:S(2)}) async-start(), calls=%async_computation | async-start | bytes 5242880 | tf_op jit(solution)/shard_map/all_gather | solution.py:60
  10.1 119.5 %all-reduce.4.cloned.1.call-start = ((), (), s32[]{:S(2)}) async-start(), calls=%async_computation.1 | async-start | bytes 1048576 | tf_op jit(solution)/shard_map/psum | solution.py:46
  57.1 460.8 %all-gather.6.cloned.1.call-start = ((), (), s32[]{:S(2)}) async-start(), calls=%async_computation.2 | async-start | bytes 5242880 | tf_op jit(solution)/shard_map/all_gather | solution.py:69
  132.6 0.8 copy-start.2
  133.4 115.2 %copy-start = (f32[2,256,256]{2,1,0:T(8,128)S(1)}, f32[2,256,256]{2,1,0:T(8,128)}, u32[]{:S(2)}) copy-start(f32[2,256,256]{2,1,0:T(8,128)} %all-reduce.4.cloned.1.call-done) | copy-start | bytes 1572868
  250.6 0.8 copy-start.3
  484.0 115.9 %all-reduce.6.cloned.1.call-start = ((), (), s32[]{:S(2)}) async-start(), calls=%async_computation.3 | async-start | bytes 1048576 | tf_op jit(solution)/shard_map/psum | solution.py:46
  527.3 460.3 %all-gather.8.cloned.1.call-start = ((), (), s32[]{:S(2)}) async-start(), calls=%async_computation.4 | async-start | bytes 5242880 | tf_op jit(solution)/shard_map/all_gather | solution.py:82
  602.9 0.8 copy-start.4
  603.7 114.9 %copy-start.1 = (f32[2,256,256]{2,1,0:T(8,128)S(1)}, f32[2,256,256]{2,1,0:T(8,128)}, u32[]{:S(2)}) copy-start(f32[2,256,256]{2,1,0:T(8,128)} %all-reduce.6.cloned.1.call-done) | copy-start | bytes 1572868
  720.6 0.8 copy-start.5
Sparse Core Ops, SparseCore 0:
  10.2 37.1 all-gather.3
  57.2 72.3 all-reduce.3
  484.1 33.7 all-gather.5
  527.5 72.3 all-reduce.5
  953.9 33.7 all-gather.7
where the time goes:
time: 1030 us; the launch traced here: 1020 us
  other arithmetic  642 us (62%)
  waiting for transfers between devices  250 us (24%)
  matrix products  57.7 us (6%)
  local copies, waits for them, and re-layouts  37.7 us (4%)
  blocking collectives  21.4 us (2%)
  between operations  15.2 us (1%)
    another operation x49, other arithmetic, orthogonal_factor(): factor_lower = jnp.linalg.cholesky(inner)  403 us
    another operation x14, other arithmetic, orthogonal_factor(): jax.scipy.linalg.solve_triangular(factor_lower, jnp.swapaxes(image, -1, -...  238 us
    psum x2, waiting for transfers between devices, whole_gram(): return lax.psum(partial_gram, 'row')  145 us
    all_gather x3, waiting for transfers between devices, shards(): lax.all_gather(blocks, 'pair', axis=1, tiled=True)  105 us
    another operation x43, local copies, waits for them, and re-layouts, orthogonal_factor(): jax.scipy.linalg.solve_triangular(factor_lower, jnp.swapaxes(image, -1, -...  24.6 us
    psum x1, blocking collectives, shards(): squares = lax.psum(jnp.sum(blocks * blocks, axis=0), 'row')  21.4 us
  transfers between devices with their start and end apart: 5, of which 5 were waited for; matrix products, arithmetic and copies ran while one was open for 0% of the time, Pallas kernels for 0%

commit v1 on v0

v1 whole, which is shorter than its diff:
```python
import functools

import jax
import jax.numpy as jnp
from jax import lax
from jax.experimental import pallas as pl
from jax.experimental.pallas import tpu as pltpu
from jax.sharding import PartitionSpec as P

BLOCK = 128
ROUNDS = 2
EIG_ITERS = 3
SUB = 8

precise = lax.Precision.HIGHEST
epsilon = 1e-06
VMEM_LIMIT = 48 * 1024 * 1024


def mm(a, b):
    return lax.dot_general(
        a, b, (((1,), (0,)), ((), ())), precision=precise, preferred_element_type=jnp.float32
    )


def mm_nt(a, b):
    return lax.dot_general(
        a, b, (((1,), (1,)), ((), ())), precision=precise, preferred_element_type=jnp.float32
    )


def mm_tn(a, b):
    return lax.dot_general(
        a, b, (((0,), (0,)), ((), ())), precision=precise, preferred_element_type=jnp.float32
    )


def sub_row(v, t):
    return jnp.broadcast_to(v[t : t + 1, :], v.shape)


def lane_col(v, l):
    return jnp.broadcast_to(v[:, l : l + 1], v.shape)


def inverse_factor(matrix):
    groups = BLOCK // SUB
    shape = (SUB, BLOCK)
    sub = lax.broadcasted_iota(jnp.int32, shape, 0)
    lane = lax.broadcasted_iota(jnp.int32, shape, 1)
    strips = [matrix[SUB * g : SUB * (g + 1), :] for g in range(groups)]
    out = []
    for k in range(groups):
        first = SUB * k
        inside = (lane >= first) & (lane < first + SUB)
        strip = strips[k]
        cols = [lane_col(strip, first + s) for s in range(SUB)]
        below = {g: [lane_col(strips[g], first + s) for s in range(SUB)] for g in range(k + 1, groups)}
        strip = jnp.where(inside, jnp.where(lane == sub + first, 1.0, 0.0), strip)
        pivots = jnp.zeros(shape, jnp.float32)
        recips, scalars, rows = [], [], []
        for t in range(SUB):
            pivot = sub_row(cols[t], t)
            recip = 1.0 / pivot
            pivots = jnp.where(sub == t, pivot, pivots)
            masked = jnp.where(sub > t, cols[t], 0.0)
            row = sub_row(strip, t)
            scalar = {}
            for s in range(t + 1, SUB):
                scalar[s] = sub_row(cols[s], t)
                cols[s] = cols[s] - (masked * scalar[s]) * recip
            if t < SUB - 1:
                strip = strip - (masked * recip) * row
            recips.append(recip)
            scalars.append(scalar)
            rows.append(row)
        for g in range(k + 1, groups):
            col = below[g]
            rest = jnp.where(inside, 0.0, strips[g])
            for t in range(SUB):
                factor = col[t] * recips[t]
                for s in range(t + 1, SUB):
                    col[s] = col[s] - factor * scalars[t][s]
                rest = rest - factor * rows[t]
            strips[g] = rest
        out.append(jnp.where(lane < first + SUB, strip, 0.0) * lax.rsqrt(pivots))
    return jnp.concatenate(out, axis=0)


def step(gram, turned):
    image = gram if turned is None else mm(turned, gram)
    inner = mm_nt(image, image)
    upper_inv = inverse_factor(inner[:BLOCK, :BLOCK])
    corner = mm_nt(inner[BLOCK:, :BLOCK], upper_inv)
    lower_inv = inverse_factor(inner[BLOCK:, BLOCK:] - mm_nt(corner, corner))
    first = mm(upper_inv, image[:BLOCK])
    second = mm(lower_inv, image[BLOCK:] - mm(corner, first))
    return first, second


def store_step(out_ref, gram, turned):
    first, second = step(gram, turned)
    out_ref[:BLOCK, :] = first
    out_ref[BLOCK:, :] = second


def opening_kernel(parts_ref, gram_ref, out_ref):
    a11, a12, a22 = parts_ref[:BLOCK], parts_ref[BLOCK : 2 * BLOCK], parts_ref[2 * BLOCK :]
    gram_ref[:BLOCK, :BLOCK] = a11
    gram_ref[:BLOCK, BLOCK:] = a12
    gram_ref[BLOCK:, :BLOCK] = a12.T
    gram_ref[BLOCK:, BLOCK:] = a22
    store_step(out_ref, gram_ref[...], None)


def step_kernel(gram_ref, turned_ref, out_ref):
    store_step(out_ref, gram_ref[...], turned_ref[...])


def last_kernel(total_rows, gram_ref, turned_ref, out_ref, spec_ref):
    gram = gram_ref[...]
    first, second = step(gram, turned_ref[...])
    turned = jnp.concatenate([first, second], axis=0)
    squares = mm_nt(mm(turned, gram), turned)
    order = 2 * BLOCK
    diagonal = lax.broadcasted_iota(jnp.int32, (order, order), 0) == lax.broadcasted_iota(
        jnp.int32, (order, order), 1
    )
    squares = jnp.where(diagonal, squares, 0.0)
    along_rows = jnp.sqrt(jnp.sum(squares, axis=1, keepdims=True) / total_rows + epsilon)
    along_lanes = jnp.sqrt(jnp.sum(squares, axis=0, keepdims=True) / total_rows + epsilon)
    out_ref[...] = turned / along_rows
    spec_ref[...] = jnp.broadcast_to(along_lanes, spec_ref.shape)


def fetch_all(copies):
    for copy in copies:
        copy.start()
    for copy in copies:
        copy.wait()


def block_copies(parts, held, sems, place, slots):
    copies = []
    for d, part in enumerate(parts):
        for j in range(slots):
            copies.append(
                pltpu.make_async_copy(
                    part.at[:, j * BLOCK : (j + 1) * BLOCK],
                    held.at[(place ^ d) * slots + j],
                    sems.at[d * slots + j],
                )
            )
    return copies


def own_gram_kernel(slots, table, *refs):
    *parts, out_ref, held, sems = refs
    place = table[4, 0]
    fetch_all(block_copies(parts, held, sems, place, slots))
    for s in range(slots // 2):
        pair = place * (slots // 2) + s
        lead, trail = held[table[0, 2 * pair]], held[table[0, 2 * pair + 1]]
        out_ref[s, :BLOCK] = mm_tn(lead, lead)
        out_ref[s, BLOCK : 2 * BLOCK] = mm_tn(lead, trail)
        out_ref[s, 2 * BLOCK :] = mm_tn(trail, trail)


def cross_gram_kernel(slots, table, *refs):
    *parts, out_ref, held, sems = refs
    place = table[4, 0]
    fetch_all(block_copies(parts, held, sems, place, slots))
    for s in range(slots // 2):
        pair = place * (slots // 2) + s
        sides = []
        for side in range(2):
            source = table[2, table[1, 2 * pair + side]] // 2
            sides.append([held[table[0, 2 * source]], held[table[0, 2 * source + 1]]])
        for i in range(2):
            for j in range(2):
                out_ref[s, i * BLOCK : (i + 1) * BLOCK, j * BLOCK : (j + 1) * BLOCK] = mm_tn(
                    sides[0][i], sides[1][j]
                )


def joint_gram_kernel(count, table, *refs):
    turned_parts, gram_parts = refs[:count], refs[count : 2 * count]
    cross_ref, out_ref, turned, grams, sems = refs[2 * count :]
    owner = table[4, 1]
    copies = []
    for d in range(count):
        copies.append(pltpu.make_async_copy(turned_parts[d], turned.at[owner ^ d], sems.at[d]))
        copies.append(pltpu.make_async_copy(gram_parts[d], grams.at[owner ^ d], sems.at[count + d]))
    fetch_all(copies)
    halves = []
    for side in range(2):
        slot = table[2, table[1, 2 * owner + side]]
        source = slot // 2
        start = pl.multiple_of((slot % 2) * BLOCK, BLOCK)
        half = turned[source, pl.ds(start, BLOCK), :]
        halves.append(half)
        a11 = grams[source, :BLOCK]
        a12 = grams[source, BLOCK : 2 * BLOCK]
        a22 = grams[source, 2 * BLOCK :]
        whole = jnp.concatenate(
            [jnp.concatenate([a11, a12], axis=1), jnp.concatenate([a12.T, a22], axis=1)], axis=0
        )
        out_ref[2 * side * BLOCK : (2 * side + 1) * BLOCK] = mm_nt(mm(half, whole), half)
    out_ref[BLOCK : 2 * BLOCK] = mm_nt(mm(halves[0], cross_ref[...]), halves[1])


def first_turn_kernel(slots, count, table, *refs):
    parts, turned_parts = refs[: count // 2], refs[count // 2 : count // 2 + count]
    out_ref, held, turned, sems = refs[count // 2 + count :]
    place, owner = table[4, 0], table[4, 1]
    copies = block_copies(parts, held, sems, place, slots)
    for d in range(count):
        copies.append(
            pltpu.make_async_copy(turned_parts[d], turned.at[owner ^ d], sems.at[len(parts) * slots + d])
        )
    fetch_all(copies)
    for j in range(slots):
        pair = table[3, place * slots + j] // 2
        for side in range(2):
            slot = table[2, table[1, 2 * pair + side]]
            source = slot // 2
            start = pl.multiple_of((slot % 2) * BLOCK, BLOCK)
            half = turned[source, pl.ds(start, BLOCK), :]
            lead, trail = held[table[0, 2 * source]], held[table[0, 2 * source + 1]]
            out_ref[j, :, side * BLOCK : (side + 1) * BLOCK] = mm_nt(lead, half[:, :BLOCK]) + mm_nt(
                trail, half[:, BLOCK:]
            )


def last_turn_kernel(slots, count, table, *refs):
    columns_ref = refs[0]
    turned_parts, spec_parts = refs[1 : 1 + count], refs[1 + count : 1 + 2 * count]
    left_ref, spec_ref, turned, spec, sems = refs[1 + 2 * count :]
    place, owner = table[4, 0], table[4, 1]
    copies = []
    for d in range(count):
        copies.append(pltpu.make_async_copy(turned_parts[d], turned.at[owner ^ d], sems.at[d]))
        copies.append(pltpu.make_async_copy(spec_parts[d], spec.at[owner ^ d], sems.at[count + d]))
    fetch_all(copies)
    for j in range(slots):
        slot = table[3, place * slots + j]
        pair = slot // 2
        start = pl.multiple_of((slot % 2) * BLOCK, BLOCK)
        left_ref[:, j * BLOCK : (j + 1) * BLOCK] = mm_nt(
            columns_ref[j], turned[pair, pl.ds(start, BLOCK), :]
        )
        spec_ref[:, j * BLOCK : (j + 1) * BLOCK] = spec[pair, :, pl.ds(start, BLOCK)]


def exchange(x, axis, bit):
    size = lax.axis_size(axis)
    return lax.ppermute(x, axis, [(i, i ^ bit) for i in range(size)])


def gather_pairwise(x):
    parts = [x]
    bit = lax.axis_size("pair") // 2
    far = []
    while bit:
        fresh = [exchange(part, "pair", bit) for part in parts]
        far.append((bit, fresh))
        parts = parts + fresh
        bit //= 2
    order = [0]
    for bit, fresh in far:
        order = order + [o ^ bit for o in order]
    return [parts[order.index(d)] for d in range(len(parts))]


def gather_owners(x):
    parts = [x, exchange(x, "row", 1)]
    result = {0: parts[0], 1: parts[1]}
    bit = lax.axis_size("pair") // 2
    while bit:
        for d, part in list(result.items()):
            result[d ^ (2 * bit)] = exchange(part, "pair", bit)
        bit //= 2
    return [result[d] for d in range(len(result))]


def sum_rows(both, low):
    own = lax.dynamic_index_in_dim(both, low, keepdims=False)
    other = lax.dynamic_index_in_dim(both, 1 - low, keepdims=False)
    total = own + exchange(other, "row", 1)
    bit = 2
    while bit < lax.axis_size("row"):
        total = total + exchange(total, "row", bit)
        bit *= 2
    return total


vmem = pl.BlockSpec(memory_space=pltpu.VMEM)
smem = pl.BlockSpec(memory_space=pltpu.SMEM)
hbm = pl.BlockSpec(memory_space=pl.ANY)


def call(kernel, in_specs, out_shapes, scratch=(), name=None, flops=0):
    return pl.pallas_call(
        kernel,
        out_shape=[jax.ShapeDtypeStruct(s, jnp.float32) for s in out_shapes],
        in_specs=in_specs,
        out_specs=[vmem] * len(out_shapes),
        scratch_shapes=list(scratch),
        compiler_params=pltpu.CompilerParams(vmem_limit_bytes=VMEM_LIMIT),
        cost_estimate=pl.CostEstimate(flops=flops, bytes_accessed=1 << 20, transcendentals=0),
        name=name,
    )


def shards(snapshots, pairing):
    rows_dev, cols_dev = snapshots.shape
    slots = cols_dev // BLOCK
    places = lax.axis_size("pair")
    blocks = places * slots
    count = 2 * places
    total_rows = rows_dev * lax.axis_size("row")
    order = 2 * BLOCK
    place = lax.axis_index("pair")
    low = lax.axis_index("row") % 2
    owner = place * 2 + low
    ids = jnp.arange(blocks, dtype=jnp.int32)
    where = jnp.sum(
        jnp.where(pairing[:, :, None] == ids[None, None, :], ids[None, :, None], 0), axis=1
    ).astype(jnp.int32)
    own_ids = jnp.where(ids == 0, place, jnp.where(ids == 1, owner, 0)).astype(jnp.int32)
    table = jnp.concatenate([pairing, where, own_ids[None]], axis=0)

    f32 = jnp.float32
    held = pltpu.VMEM((blocks, rows_dev, BLOCK), f32)
    parts = gather_pairwise(snapshots)
    dma = pltpu.SemaphoreType.DMA
    half = slots // 2
    (own_grams,) = call(
        functools.partial(own_gram_kernel, slots),
        [smem] + [hbm] * places,
        [(half, 3 * BLOCK, BLOCK)],
        [held, dma((blocks,))],
        "own_gram",
    )(table, *parts)
    (cross_grams,) = call(
        functools.partial(cross_gram_kernel, slots),
        [smem] + [hbm] * places,
        [(half, order, order)],
        [held, dma((blocks,))],
        "cross_gram",
    )(table, *parts)
    own_gram = sum_rows(own_grams, low)
    cross_gram = sum_rows(cross_grams, low)
    gram_parts = gather_owners(own_gram)

    chain = 1 << 33
    square = (order, order)

    def rotate(gram_pieces, last):
        gram, turned = call(opening_kernel, [vmem], [square, square], (), "opening_step", chain)(gram_pieces)
        for iteration in range(1, EIG_ITERS):
            if last and iteration == EIG_ITERS - 1:
                return call(
                    functools.partial(last_kernel, total_rows),
                    [vmem, vmem],
                    [square, (SUB, order)],
                    (),
                    "last_step",
                    chain,
                )(gram, turned)
            (turned,) = call(step_kernel, [vmem, vmem], [square], (), "inner_step", chain)(gram, turned)
        return turned

    turned = rotate(own_gram, False)
    turned_parts = gather_owners(turned)
    (joint_gram,) = call(
        functools.partial(joint_gram_kernel, count),
        [smem] + [hbm] * (2 * count) + [vmem],
        [(3 * BLOCK, BLOCK)],
        [
            pltpu.VMEM((count,) + square, f32),
            pltpu.VMEM((count, 3 * BLOCK, BLOCK), f32),
            dma((2 * count,)),
        ],
        "joint_gram",
    )(table, *turned_parts, *gram_parts, cross_gram)
    second, spec = rotate(joint_gram, True)
    (columns,) = call(
        functools.partial(first_turn_kernel, slots, count),
        [smem] + [hbm] * (places + count),
        [(slots, rows_dev, order)],
        [held, pltpu.VMEM((count,) + square, f32), dma((blocks + count,))],
        "first_turn",
    )(table, *parts, *turned_parts)
    second_parts = gather_owners(second)
    spec_parts = gather_owners(spec)
    left, spectrum = call(
        functools.partial(last_turn_kernel, slots, count),
        [smem, vmem] + [hbm] * (2 * count),
        [(rows_dev, cols_dev), (SUB, cols_dev)],
        [
            pltpu.VMEM((count,) + square, f32),
            pltpu.VMEM((count, SUB, order), f32),
            dma((2 * count,)),
        ],
        "last_turn",
    )(table, columns, *second_parts, *spec_parts)
    return left, spectrum[0]


def solution(mesh):
    return jax.shard_map(
        shards,
        mesh=mesh,
        in_specs=(P("row", "pair"), P()),
        out_specs=(P("row", "pair"), P("pair")),
        check_vma=False,
    )
```

time: 1030 us -> 196 us (0.19)
  other arithmetic: 642 us -> 3.5 us
  waiting for transfers between devices: 250 us -> 72.7 us
  Pallas kernels: 0 us -> 79.5 us
  matrix products: 57.7 us -> 0 us
  local copies, waits for them, and re-layouts: 37.7 us -> 4.88 us
  starting transfers between devices: 0.42 us -> 31 us
  blocking collectives: 21.4 us -> 0 us
  between operations: 15.2 us -> 1.14 us
    another operation x63 -> x0, other arithmetic: 641 us -> none  [the longest x49 403 us: orthogonal_factor(): factor_lower = jnp.linalg.cholesky(inner)]
    psum x2 -> x0, waiting for transfers between devices: 145 us -> none  [whole_gram(): return lax.psum(partial_gram, 'row')]
    all_gather x3 -> x0, waiting for transfers between devices: 105 us -> none  [shards(): lax.all_gather(blocks, 'pair', axis=1, tiled=True)]
    pallas_call x0 -> x11, Pallas kernels: none -> 79.5 us  [the longest x3 29.3 us: rotate(): call(step_kernel, [vmem, vmem], [square], (), 'inner_step', chain)]
    ppermute x0 -> x37, waiting for transfers between devices: none -> 72.7 us  [exchange(): return lax.ppermute(x, axis, [(i, i ^ bit) for i in range(size)])]
    dot_general x19 -> x0, matrix products: 37.9 us -> none  [the longest x3 18.1 us: folding(): jnp.einsum('rnc,nk->rkc', segment, selection, precision=precise)]
    ppermute x0 -> x37, starting transfers between devices: none -> 31 us  [exchange(): return lax.ppermute(x, axis, [(i, i ^ bit) for i in range(size)])]
    another operation x55 -> x0, local copies, waits for them, and re-layouts: 24.8 us -> none  [the longest x43 24.6 us: orthogonal_factor(): jax.scipy.linalg.solve_triangular(factor_lower, jnp.swapaxes(image, -1, -...]
  transfers between devices with their start and end apart: 5 -> 37, of which waited for: 5 -> 20; matrix products, arithmetic and copies ran while one was open for 0% -> 2% of each run, Pallas kernels for 0% -> 20%
where the time goes in v1:
time: 196 us; the launch traced here: 193 us
  Pallas kernels  79.5 us (41%)
  waiting for transfers between devices  72.7 us (37%)
  starting transfers between devices  31 us (16%)
  local copies, waits for them, and re-layouts  4.88 us (2%)
  other arithmetic  3.5 us (2%)
    ppermute x37, waiting for transfers between devices, exchange(): return lax.ppermute(x, axis, [(i, i ^ bit) for i in range(size)])  72.7 us
    ppermute x37, starting transfers between devices, exchange(): return lax.ppermute(x, axis, [(i, i ^ bit) for i in range(size)])  31 us
    pallas_call x3, Pallas kernels, rotate(): call(step_kernel, [vmem, vmem], [square], (), 'inner_step', chain)  29.3 us
    pallas_call x2, Pallas kernels, rotate(): call(opening_kernel, [vmem], [square, square], (), 'opening_step', chain)  18.2 us
    pallas_call x1, Pallas kernels, rotate(): call(functools.partial(last_kernel, total_rows), [vmem, vmem], [square, (...  10.6 us
    pallas_call x1, Pallas kernels, shards(): call(functools.partial(first_turn_kernel, slots, count), [smem] + [hbm] *...  7.29 us
    pallas_call x1, Pallas kernels, shards(): call(functools.partial(joint_gram_kernel, count), [smem] + [hbm] * (2 * c...  4.15 us
  transfers between devices with their start and end apart: 37, of which 20 were waited for; matrix products, arithmetic and copies ran while one was open for 2% of the time, Pallas kernels for 20%

profile of v1, /device:TPU:0, one launch (start us, length us, event | category | flops | bytes accessed | tf_op | source)
XLA Modules:
  0.0 192.8 jit_solution(10291513315788703873)
XLA Ops:
  0.6 3.0 %collective-permute-start.1 = (f32[512,512]{1,0:T(8,128)}, f32[512,512]{1,0:T(8,128)S(1)}, u32[]{:S(2)}, u32[]{:S(2)}) collective-permute-start(f32[512,512]{1,0:T(8,128)} %refs_0_.5), channel_id=1, source_target_pairs={{0,2},{1,3},{2,0},{3,1},{4,6},{5,7},{6,4},{7,5},{8,10},{9,11},{10,... | collective-permute-start | bytes 3145736 | tf_op jit(solution)/shard_map/ppermute | solution.py:257
  3.7 23.4 %collective-permute-done.1.refs_2_ = f32[512,512]{1,0:T(8,128)S(1)} collective-permute-done((f32[512,512]{1,0:T(8,128)}, f32[512,512]{1,0:T(8,128)S(1)}, u32[]{:S(2)}, u32[]{:S(2)}) %collective-permute-start.1) | collective-permute-done | bytes 1048608 | tf_op jit(solution)/shard_map/ppermute | solution.py:257
  30.9 2.8 %own_gram.1 = f32[2,384,128]{2,1,0:T(8,128)S(1)} custom-call(s32[5,16]{1,0:T(8,128)S(1)} %pad_add_fusion.table, f32[512,512]{1,0:T(8,128)S(1)} %copy-done, f32[512,512]{1,0:T(8,128)S(1)} %collective-permute-done.refs_1_, f32[512,512]{1,0:T(8,128)S(1)} %collective-permute-done.1.refs_2_, f32[512,512]{1,0:T(8,128)S(1)} %collective-permute-done.2.refs_3_), custom_call_target="tpu_custom_call" | custom-call | bytes 1048576 | tf_op jit(solution)/shard_map/own_gram/pallas_call | solution.py:338
  36.1 3.4 %cross_gram.1 = f32[2,256,256]{2,1,0:T(8,128)S(1)} custom-call(s32[5,16]{1,0:T(8,128)S(1)} %pad_add_fusion.table, f32[512,512]{1,0:T(8,128)S(1)} %copy-done, f32[512,512]{1,0:T(8,128)S(1)} %collective-permute-done.refs_1_, f32[512,512]{1,0:T(8,128)S(1)} %collective-permute-done.1.refs_2_, f32[512,512]{1,0:T(8,128)S(1)} %collective-permute-done.2.refs_3_), custom_call_target="tpu_custom_call" | custom-call | bytes 1048576 | tf_op jit(solution)/shard_map/cross_gram/pallas_call | solution.py:345
  44.5 4.0 %collective-permute-done.20 = f32[256,256]{1,0:T(8,128)S(1)} collective-permute-done((f32[256,256]{1,0:T(8,128)S(1)}, f32[256,256]{1,0:T(8,128)S(1)}, u32[]{:S(2)}, u32[]{:S(2)}) %collective-permute-start.20) | collective-permute-done | bytes 262176 | tf_op jit(solution)/shard_map/ppermute | solution.py:257
  51.1 2.7 %collective-permute-start.5 = (f32[384,128]{1,0:T(8,128)S(1)}, f32[384,128]{1,0:T(8,128)S(1)}, u32[]{:S(2)}, u32[]{:S(2)}) collective-permute-start(f32[384,128]{1,0:T(8,128)S(1)} %add.41), channel_id=1, source_target_pairs={{0,16},{4,20},{8,24},{12,28},{16,0},{20,4},{24,8},{28,12},{1,17},{... | collective-permute-start | bytes 589832 | tf_op jit(solution)/shard_map/ppermute | solution.py:257
  53.8 7.2 %collective-permute-done.21 = f32[256,256]{1,0:T(8,128)S(1)} collective-permute-done((f32[256,256]{1,0:T(8,128)S(1)}, f32[256,256]{1,0:T(8,128)S(1)}, u32[]{:S(2)}, u32[]{:S(2)}) %collective-permute-start.21) | collective-permute-done | bytes 262176 | tf_op jit(solution)/shard_map/ppermute | solution.py:257
  62.8 9.1 %opening_step.2 = (f32[256,256]{1,0:T(8,128)S(1)}, f32[256,256]{1,0:T(8,128)S(1)}) custom-call(f32[384,128]{1,0:T(8,128)S(1)} %add.42.parts_ref.refs_8_), custom_call_target="tpu_custom_call" | custom-call | flops 8589934592 | bytes 1048576 | tf_op jit(solution)/shard_map/opening_step/pallas_call | solution.py:360
  71.8 9.9 %inner_step.3.turned_ref = f32[256,256]{1,0:T(8,128)S(1)} custom-call(f32[256,256]{1,0:T(8,128)S(1)} %get-tuple-element.10.gram_ref, f32[256,256]{1,0:T(8,128)S(1)} %get-tuple-element.11.turned_ref), custom_call_target="tpu_custom_call" | custom-call | flops 8589934592 | bytes 1048576 | tf_op jit(solution)/shard_map/inner_step/pallas_call | solution.py:371
  81.8 9.7 %inner_step.4.refs_4_.refs_0_ = f32[256,256]{1,0:T(8,128)S(1)} custom-call(f32[256,256]{1,0:T(8,128)S(1)} %get-tuple-element.10.gram_ref, f32[256,256]{1,0:T(8,128)S(1)} %inner_step.3.turned_ref), custom_call_target="tpu_custom_call" | custom-call | flops 8589934592 | bytes 1048576 | tf_op jit(solution)/shard_map/inner_step/pallas_call | solution.py:371
  95.6 2.1 %collective-permute-done.16.refs_12_ = f32[384,128]{1,0:T(8,128)S(1)} collective-permute-done((f32[384,128]{1,0:T(8,128)S(1)}, f32[384,128]{1,0:T(8,128)S(1)}, u32[]{:S(2)}, u32[]{:S(2)}) %collective-permute-start.16) | collective-permute-done | bytes 196640 | tf_op jit(solution)/shard_map/ppermute | solution.py:257
  104.7 5.1 %collective-permute-done.10.refs_9_.refs_5_ = f32[256,256]{1,0:T(8,128)S(1)} collective-permute-done((f32[256,256]{1,0:T(8,128)S(1)}, f32[256,256]{1,0:T(8,128)S(1)}, u32[]{:S(2)}, u32[]{:S(2)}) %collective-permute-start.10) | collective-permute-done | bytes 262176 | tf_op jit(solution)/shard_map/ppermute | solution.py:257
  110.3 3.0 %collective-permute-done.17.refs_13_ = f32[384,128]{1,0:T(8,128)S(1)} collective-permute-done((f32[384,128]{1,0:T(8,128)S(1)}, f32[384,128]{1,0:T(8,128)S(1)}, u32[]{:S(2)}, u32[]{:S(2)}) %collective-permute-start.17) | collective-permute-done | bytes 196640 | tf_op jit(solution)/shard_map/ppermute | solution.py:257
  114.8 4.1 %joint_gram.1.parts_ref = f32[384,128]{1,0:T(8,128)S(1)} custom-call(s32[5,16]{1,0:T(8,128)S(1)} %pad_add_fusion.table, f32[256,256]{1,0:T(8,128)S(1)} %inner_step.4.refs_4_.refs_0_, f32[256,256]{1,0:T(8,128)S(1)} %collective-permute-done.6.refs_5_.refs_1_, f32[256,256]{1,0:T(8,128)S(1)} %collective-permute-done.7.refs_6_.refs_2_, ...), custom_call_target="tpu_custom_call" | custom-call | bytes 1048576 | tf_op jit(solution)/shard_map/joint_gram/pallas_call | solution.py:376
  118.9 9.1 %opening_step.3 = (f32[256,256]{1,0:T(8,128)S(1)}, f32[256,256]{1,0:T(8,128)S(1)}) custom-call(f32[384,128]{1,0:T(8,128)S(1)} %joint_gram.1.parts_ref), custom_call_target="tpu_custom_call" | custom-call | flops 8589934592 | bytes 1048576 | tf_op jit(solution)/shard_map/opening_step/pallas_call | solution.py:360
  128.0 9.7 %inner_step.5.turned_ref = f32[256,256]{1,0:T(8,128)S(1)} custom-call(f32[256,256]{1,0:T(8,128)S(1)} %get-tuple-element.12.gram_ref, f32[256,256]{1,0:T(8,128)S(1)} %get-tuple-element.13.turned_ref), custom_call_target="tpu_custom_call" | custom-call | flops 8589934592 | bytes 1048576 | tf_op jit(solution)/shard_map/inner_step/pallas_call | solution.py:371
  137.8 10.6 %last_step.1 = (f32[256,256]{1,0:T(8,128)S(1)}, f32[8,256]{1,0:T(8,128)S(1)}) custom-call(f32[256,256]{1,0:T(8,128)S(1)} %get-tuple-element.12.gram_ref, f32[256,256]{1,0:T(8,128)S(1)} %inner_step.5.turned_ref), custom_call_target="tpu_custom_call" | custom-call | flops 8589934592 | bytes 1048576 | tf_op jit(solution)/shard_map/last_step/pallas_call | solution.py:363
  151.2 5.5 %collective-permute-done.23.refs_2_ = f32[256,256]{1,0:T(8,128)S(1)} collective-permute-done((f32[256,256]{1,0:T(8,128)S(1)}, f32[256,256]{1,0:T(8,128)S(1)}, u32[]{:S(2)}, u32[]{:S(2)}) %collective-permute-start.23) | collective-permute-done | bytes 262176 | tf_op jit(solution)/shard_map/ppermute | solution.py:257
  158.6 5.6 %collective-permute-done.27.refs_6_ = f32[256,256]{1,0:T(8,128)S(1)} collective-permute-done((f32[256,256]{1,0:T(8,128)S(1)}, f32[256,256]{1,0:T(8,128)S(1)}, u32[]{:S(2)}, u32[]{:S(2)}) %collective-permute-start.27) | collective-permute-done | bytes 262176 | tf_op jit(solution)/shard_map/ppermute | solution.py:257
  165.6 2.3 %collective-permute-done.33.refs_13_ = f32[8,256]{1,0:T(8,128)S(1)} collective-permute-done((f32[8,256]{1,0:T(8,128)S(1)}, f32[8,256]{1,0:T(8,128)S(1)}, u32[]{:S(2)}, u32[]{:S(2)}) %collective-permute-start.33) | collective-permute-done | bytes 8224 | tf_op jit(solution)/shard_map/ppermute | solution.py:257
  170.6 2.3 %collective-permute-done.30.refs_10_ = f32[8,256]{1,0:T(8,128)S(1)} collective-permute-done((f32[8,256]{1,0:T(8,128)S(1)}, f32[8,256]{1,0:T(8,128)S(1)}, u32[]{:S(2)}, u32[]{:S(2)}) %collective-permute-start.30) | collective-permute-done | bytes 8224 | tf_op jit(solution)/shard_map/ppermute | solution.py:257
  175.5 2.3 %collective-permute-done.34.refs_14_ = f32[8,256]{1,0:T(8,128)S(1)} collective-permute-done((f32[8,256]{1,0:T(8,128)S(1)}, f32[8,256]{1,0:T(8,128)S(1)}, u32[]{:S(2)}, u32[]{:S(2)}) %collective-permute-start.34) | collective-permute-done | bytes 8224 | tf_op jit(solution)/shard_map/ppermute | solution.py:257
  179.1 7.3 %first_turn.1.refs_0_ = f32[4,512,256]{2,1,0:T(8,128)} custom-call(s32[5,16]{1,0:T(8,128)S(1)} %pad_add_fusion.table, f32[512,512]{1,0:T(8,128)S(1)} %copy-done.1, f32[512,512]{1,0:T(8,128)S(1)} %collective-permute-done.refs_1_, f32[512,512]{1,0:T(8,128)S(1)} %collective-permute-done.1.refs_2_, f32[512,512]{1,0:T(8,128)} %copy-done.2, ...), custom_call_target="tpu_custom_call" | custom-call | bytes 1048576 | tf_op jit(solution)/shard_map/first_turn/pallas_call | solution.py:388
  188.1 3.9 %last_turn.1 = (f32[512,512]{1,0:T(8,128)}, f32[8,512]{1,0:T(8,128)S(1)}) custom-call(s32[5,16]{1,0:T(8,128)S(1)} %pad_add_fusion.table, f32[4,512,256]{2,1,0:T(8,128)S(1)} %copy-done.3, f32[256,256]{1,0:T(8,128)S(1)} %get-tuple-element.14.refs_1_, f32[256,256]{1,0:T(8,128)S(1)} %collective-permute-done.23.refs_2_, ...), custom_call_target="tpu_custom_call" | custom-call | bytes 1048576 | tf_op jit(solution)/shard_map/last_turn/pallas_call | solution.py:397
  (83 shorter events, 43.6 us)
Async XLA Ops:
  0.6 26.4 %collective-permute-start.1 = (f32[512,512]{1,0:T(8,128)}, f32[512,512]{1,0:T(8,128)S(1)}, u32[]{:S(2)}, u32[]{:S(2)}) collective-permute-start(f32[512,512]{1,0:T(8,128)} %refs_0_.5), channel_id=1, source_target_pairs={{0,2},{1,3},{2,0},{3,1},{4,6},{5,7},{6,4},{7,5},{8,10},{9,11},{10,... | collective-permute-start | bytes 3145736 | tf_op jit(solution)/shard_map/ppermute | solution.py:257
  3.7 24.8 %collective-permute-start = (f32[512,512]{1,0:T(8,128)}, f32[512,512]{1,0:T(8,128)S(1)}, u32[]{:S(2)}, u32[]{:S(2)}) collective-permute-start(f32[512,512]{1,0:T(8,128)} %refs_0_.5), channel_id=1, source_target_pairs={{0,1},{1,0},{2,3},{3,2},{4,5},{5,4},{6,7},{7,6},{8,9},{9,8},{10,11... | collective-permute-start | bytes 3145736 | tf_op jit(solution)/shard_map/ppermute | solution.py:257
  40.4 8.1 %collective-permute-start.20 = (f32[256,256]{1,0:T(8,128)S(1)}, f32[256,256]{1,0:T(8,128)S(1)}, u32[]{:S(2)}, u32[]{:S(2)}) collective-permute-start(f32[256,256]{1,0:T(8,128)S(1)} %dynamic-slice_bitcast_fusion), channel_id=1, source_target_pairs={{0,4},{4,0},{8,12},{12,8},{16,20},{20,16},{24,28},{28,24},{1,5},{5... | collective-permute-start | bytes 786440 | tf_op jit(solution)/shard_map/ppermute | solution.py:257
  42.6 8.5 %collective-permute-start.4 = (f32[384,128]{1,0:T(8,128)S(1)}, f32[384,128]{1,0:T(8,128)S(1)}, u32[]{:S(2)}, u32[]{:S(2)}) collective-permute-start(f32[384,128]{1,0:T(8,128)S(1)} %bitcast_add_fusion.1), channel_id=1, source_target_pairs={{0,8},{4,12},{8,0},{12,4},{16,24},{20,28},{24,16},{28,20},{1,9},{5... | collective-permute-start | bytes 589832 | tf_op jit(solution)/shard_map/ppermute | solution.py:257
  49.5 11.5 %collective-permute-start.21 = (f32[256,256]{1,0:T(8,128)S(1)}, f32[256,256]{1,0:T(8,128)S(1)}, u32[]{:S(2)}, u32[]{:S(2)}) collective-permute-start(f32[256,256]{1,0:T(8,128)S(1)} %bitcast_add_fusion), channel_id=1, source_target_pairs={{0,8},{4,12},{8,0},{12,4},{16,24},{20,28},{24,16},{28,20},{1,9},{5... | collective-permute-start | bytes 786440 | tf_op jit(solution)/shard_map/ppermute | solution.py:257
  51.1 11.6 %collective-permute-start.5 = (f32[384,128]{1,0:T(8,128)S(1)}, f32[384,128]{1,0:T(8,128)S(1)}, u32[]{:S(2)}, u32[]{:S(2)}) collective-permute-start(f32[384,128]{1,0:T(8,128)S(1)} %add.41), channel_id=1, source_target_pairs={{0,16},{4,20},{8,24},{12,28},{16,0},{20,4},{24,8},{28,12},{1,17},{... | collective-permute-start | bytes 589832 | tf_op jit(solution)/shard_map/ppermute | solution.py:257
  61.0 34.1 %collective-permute-start.22 = (f32[256,256]{1,0:T(8,128)S(1)}, f32[256,256]{1,0:T(8,128)S(1)}, u32[]{:S(2)}, u32[]{:S(2)}) collective-permute-start(f32[256,256]{1,0:T(8,128)S(1)} %add.44), channel_id=1, source_target_pairs={{0,16},{4,20},{8,24},{12,28},{16,0},{20,4},{24,8},{28,12},{1,17},{... | collective-permute-start | bytes 786440 | tf_op jit(solution)/shard_map/ppermute | solution.py:257
  91.4 8.3 %collective-permute-start.6 = (f32[256,256]{1,0:T(8,128)S(1)}, f32[256,256]{1,0:T(8,128)S(1)}, u32[]{:S(2)}, u32[]{:S(2)}) collective-permute-start(f32[256,256]{1,0:T(8,128)S(1)} %inner_step.4.refs_4_.refs_0_), channel_id=1, source_target_pairs={{0,4},{4,0},{8,12},{12,8},{16,20},{20,16},{24,28},{28,24},{1,5},{5... | collective-permute-start | bytes 786440 | tf_op jit(solution)/shard_map/ppermute | solution.py:257
  93.6 8.3 %collective-permute-start.14 = (f32[384,128]{1,0:T(8,128)S(1)}, f32[384,128]{1,0:T(8,128)S(1)}, u32[]{:S(2)}, u32[]{:S(2)}) collective-permute-start(f32[384,128]{1,0:T(8,128)S(1)} %add.42.parts_ref.refs_8_), channel_id=1, source_target_pairs={{0,1},{1,0},{2,3},{3,2},{4,5},{5,4},{6,7},{7,6},{8,9},{9,8},{10,11... | collective-permute-start | bytes 589832 | tf_op jit(solution)/shard_map/ppermute | solution.py:257
  93.6 8.9 %collective-permute-start.13 = (f32[384,128]{1,0:T(8,128)S(1)}, f32[384,128]{1,0:T(8,128)S(1)}, u32[]{:S(2)}, u32[]{:S(2)}) collective-permute-start(f32[384,128]{1,0:T(8,128)S(1)} %add.42.parts_ref.refs_8_), channel_id=1, source_target_pairs={{0,4},{4,0},{8,12},{12,8},{16,20},{20,16},{24,28},{28,24},{1,5},{5... | collective-permute-start | bytes 589832 | tf_op jit(solution)/shard_map/ppermute | solution.py:257
  95.1 9.1 %collective-permute-start.9 = (f32[256,256]{1,0:T(8,128)S(1)}, f32[256,256]{1,0:T(8,128)S(1)}, u32[]{:S(2)}, u32[]{:S(2)}) collective-permute-start(f32[256,256]{1,0:T(8,128)S(1)} %inner_step.4.refs_4_.refs_0_), channel_id=1, source_target_pairs={{0,2},{1,3},{2,0},{3,1},{4,6},{5,7},{6,4},{7,5},{8,10},{9,11},{10,... | collective-permute-start | bytes 786440 | tf_op jit(solution)/shard_map/ppermute | solution.py:257
  99.7 10.1 %collective-permute-start.10 = (f32[256,256]{1,0:T(8,128)S(1)}, f32[256,256]{1,0:T(8,128)S(1)}, u32[]{:S(2)}, u32[]{:S(2)}) collective-permute-start(f32[256,256]{1,0:T(8,128)S(1)} %collective-permute-done.6.refs_5_.refs_1_), channel_id=1, source_target_pairs={{0,2},{1,3},{2,0},{3,1},{4,6},{5,7},{6,4},{7,5},{8,10},{9,11},{10,... | collective-permute-start | bytes 786440 | tf_op jit(solution)/shard_map/ppermute | solution.py:257
  101.8 8.0 %collective-permute-start.18 = (f32[384,128]{1,0:T(8,128)S(1)}, f32[384,128]{1,0:T(8,128)S(1)}, u32[]{:S(2)}, u32[]{:S(2)}) collective-permute-start(f32[384,128]{1,0:T(8,128)S(1)} %collective-permute-done.16.refs_12_), channel_id=1, source_target_pairs={{0,1},{1,0},{2,3},{3,2},{4,5},{5,4},{6,7},{7,6},{8,9},{9,8},{10,11... | collective-permute-start | bytes 589832 | tf_op jit(solution)/shard_map/ppermute | solution.py:257
  102.4 10.9 %collective-permute-start.17 = (f32[384,128]{1,0:T(8,128)S(1)}, f32[384,128]{1,0:T(8,128)S(1)}, u32[]{:S(2)}, u32[]{:S(2)}) collective-permute-start(f32[384,128]{1,0:T(8,128)S(1)} %collective-permute-done.13.refs_9_), channel_id=1, source_target_pairs={{0,2},{1,3},{2,0},{3,1},{4,6},{5,7},{6,4},{7,5},{8,10},{9,11},{10,... | collective-permute-start | bytes 589832 | tf_op jit(solution)/shard_map/ppermute | solution.py:257
  104.2 9.2 %collective-permute-start.11 = (f32[256,256]{1,0:T(8,128)S(1)}, f32[256,256]{1,0:T(8,128)S(1)}, u32[]{:S(2)}, u32[]{:S(2)}) collective-permute-start(f32[256,256]{1,0:T(8,128)S(1)} %collective-permute-done.9.refs_8_.refs_4_), channel_id=1, source_target_pairs={{0,1},{1,0},{2,3},{3,2},{4,5},{5,4},{6,7},{7,6},{8,9},{9,8},{10,11... | collective-permute-start | bytes 786440 | tf_op jit(solution)/shard_map/ppermute | solution.py:257
  104.2 9.2 %collective-permute-start.8 = (f32[256,256]{1,0:T(8,128)S(1)}, f32[256,256]{1,0:T(8,128)S(1)}, u32[]{:S(2)}, u32[]{:S(2)}) collective-permute-start(f32[256,256]{1,0:T(8,128)S(1)} %collective-permute-done.6.refs_5_.refs_1_), channel_id=1, source_target_pairs={{0,1},{1,0},{2,3},{3,2},{4,5},{5,4},{6,7},{7,6},{8,9},{9,8},{10,11... | collective-permute-start | bytes 786440 | tf_op jit(solution)/shard_map/ppermute | solution.py:257
  148.3 8.4 %collective-permute-start.23 = (f32[256,256]{1,0:T(8,128)S(1)}, f32[256,256]{1,0:T(8,128)S(1)}, u32[]{:S(2)}, u32[]{:S(2)}) collective-permute-start(f32[256,256]{1,0:T(8,128)S(1)} %get-tuple-element.14.refs_1_), channel_id=1, source_target_pairs={{0,4},{4,0},{8,12},{12,8},{16,20},{20,16},{24,28},{28,24},{1,5},{5... | collective-permute-start | bytes 786440 | tf_op jit(solution)/shard_map/ppermute | solution.py:257
  149.7 8.9 %collective-permute-start.26 = (f32[256,256]{1,0:T(8,128)S(1)}, f32[256,256]{1,0:T(8,128)S(1)}, u32[]{:S(2)}, u32[]{:S(2)}) collective-permute-start(f32[256,256]{1,0:T(8,128)S(1)} %get-tuple-element.14.refs_1_), channel_id=1, source_target_pairs={{0,2},{1,3},{2,0},{3,1},{4,6},{5,7},{6,4},{7,5},{8,10},{9,11},{10,... | collective-permute-start | bytes 786440 | tf_op jit(solution)/shard_map/ppermute | solution.py:257
  156.7 7.5 %collective-permute-start.27 = (f32[256,256]{1,0:T(8,128)S(1)}, f32[256,256]{1,0:T(8,128)S(1)}, u32[]{:S(2)}, u32[]{:S(2)}) collective-permute-start(f32[256,256]{1,0:T(8,128)S(1)} %collective-permute-done.23.refs_2_), channel_id=1, source_target_pairs={{0,2},{1,3},{2,0},{3,1},{4,6},{5,7},{6,4},{7,5},{8,10},{9,11},{10,... | collective-permute-start | bytes 786440 | tf_op jit(solution)/shard_map/ppermute | solution.py:257
  158.1 28.4 %collective-permute-start.24 = (f32[256,256]{1,0:T(8,128)S(1)}, f32[256,256]{1,0:T(8,128)S(1)}, u32[]{:S(2)}, u32[]{:S(2)}) collective-permute-start(f32[256,256]{1,0:T(8,128)S(1)} %get-tuple-element.14.refs_1_), channel_id=1, source_target_pairs={{0,1},{1,0},{2,3},{3,2},{4,5},{5,4},{6,7},{7,6},{8,9},{9,8},{10,11... | collective-permute-start | bytes 786440 | tf_op jit(solution)/shard_map/ppermute | solution.py:257
  158.1 28.4 %collective-permute-start.25 = (f32[256,256]{1,0:T(8,128)S(1)}, f32[256,256]{1,0:T(8,128)S(1)}, u32[]{:S(2)}, u32[]{:S(2)}) collective-permute-start(f32[256,256]{1,0:T(8,128)S(1)} %collective-permute-done.23.refs_2_), channel_id=1, source_target_pairs={{0,1},{1,0},{2,3},{3,2},{4,5},{5,4},{6,7},{7,6},{8,9},{9,8},{10,11... | collective-permute-start | bytes 786440 | tf_op jit(solution)/shard_map/ppermute | solution.py:257
  158.6 27.9 %collective-permute-start.28 = (f32[256,256]{1,0:T(8,128)S(1)}, f32[256,256]{1,0:T(8,128)S(1)}, u32[]{:S(2)}, u32[]{:S(2)}) collective-permute-start(f32[256,256]{1,0:T(8,128)S(1)} %collective-permute-done.26.refs_5_), channel_id=1, source_target_pairs={{0,1},{1,0},{2,3},{3,2},{4,5},{5,4},{6,7},{7,6},{8,9},{9,8},{10,11... | collective-permute-start | bytes 786440 | tf_op jit(solution)/shard_map/ppermute | solution.py:257
  164.3 22.2 %collective-permute-start.29 = (f32[256,256]{1,0:T(8,128)S(1)}, f32[256,256]{1,0:T(8,128)S(1)}, u32[]{:S(2)}, u32[]{:S(2)}) collective-permute-start(f32[256,256]{1,0:T(8,128)S(1)} %collective-permute-done.27.refs_6_), channel_id=1, source_target_pairs={{0,1},{1,0},{2,3},{3,2},{4,5},{5,4},{6,7},{7,6},{8,9},{9,8},{10,11... | collective-permute-start | bytes 786440 | tf_op jit(solution)/shard_map/ppermute | solution.py:257
  179.0 7.5 %collective-permute-start.36 = (f32[8,256]{1,0:T(8,128)S(1)}, f32[8,256]{1,0:T(8,128)S(1)}, u32[]{:S(2)}, u32[]{:S(2)}) collective-permute-start(f32[8,256]{1,0:T(8,128)S(1)} %collective-permute-done.34.refs_14_), channel_id=1, source_target_pairs={{0,1},{1,0},{2,3},{3,2},{4,5},{5,4},{6,7},{7,6},{8,9},{9,8},{10,11... | collective-permute-start | bytes 24584 | tf_op jit(solution)/shard_map/ppermute | solution.py:257
  (18 other events, 96.9 us)

commit v2 on v0

v2 whole, which is shorter than its diff:
```python
import functools

import jax
import jax.numpy as jnp
from jax import lax
from jax.experimental import pallas as pl
from jax.experimental.pallas import tpu as pltpu
from jax.sharding import PartitionSpec as P

BLOCK = 128
ROUNDS = 2
EIG_ITERS = 3
SUB = 8

precise = lax.Precision.HIGHEST
epsilon = 1e-06
VMEM_LIMIT = 24 * 1024 * 1024
PACK = BLOCK // 4
HALF_ROWS = BLOCK + PACK
STEP_ROWS = 2 * HALF_ROWS + SUB
PACK_PLACES = ((BLOCK, 0), (BLOCK, BLOCK), (HALF_ROWS + BLOCK, 0), (HALF_ROWS + BLOCK, BLOCK))
ALONE = (64, 2)
PAIRED = (32, 1)


def mm(a, b):
    return lax.dot_general(
        a, b, (((1,), (0,)), ((), ())), precision=precise, preferred_element_type=jnp.float32
    )


def mm_nt(a, b):
    return lax.dot_general(
        a, b, (((1,), (1,)), ((), ())), precision=precise, preferred_element_type=jnp.float32
    )


def mm_tn(a, b):
    return lax.dot_general(
        a, b, (((0,), (0,)), ((), ())), precision=precise, preferred_element_type=jnp.float32
    )


def halves_of(x):
    high = x.astype(jnp.bfloat16)
    return high, (x - high.astype(jnp.float32)).astype(jnp.bfloat16)


def mm_nt_three(a, b):
    def one(x, y):
        return lax.dot_general(x, y, (((1,), (1,)), ((), ())), preferred_element_type=jnp.float32)

    (a_high, a_low), (b_high, b_low) = halves_of(a), halves_of(b)
    return one(a_high, b_high) + (one(a_high, b_low) + one(a_low, b_high))


def sub_row(v, t):
    return jnp.broadcast_to(v[t : t + 1, :], v.shape)


def lane_col(v, l):
    return jnp.broadcast_to(v[:, l : l + 1], v.shape)


def factor_steps(matrix, panel, ahead):
    groups, strips_panel = BLOCK // SUB, panel // SUB
    shape = (SUB, BLOCK)
    sub = lax.broadcasted_iota(jnp.int32, shape, 0)
    lane = lax.broadcasted_iota(jnp.int32, shape, 1)
    strips = [matrix[SUB * g : SUB * (g + 1), :] for g in range(groups)]
    out = []
    for opening in range(0, groups, strips_panel):
        end = opening + strips_panel
        next_cols = next_below = None
        finished = []
        for k in range(opening, end):
            first = SUB * k
            inside = (lane >= first) & (lane < first + SUB)
            strip = strips[k]
            cols = next_cols
            if cols is None:
                cols = [lane_col(strip, first + s) for s in range(SUB)]
            below = {}
            for g in range(k + 1, end):
                if g == k + 1 and next_below is not None:
                    below[g] = next_below
                else:
                    below[g] = [lane_col(strips[g], first + s) for s in range(SUB)]
            next_cols = next_below = None
            if ahead >= 1 and k + 1 < end:
                next_cols = [lane_col(strips[k + 1], first + SUB + s) for s in range(SUB)]
            if ahead >= 2 and k + 2 < end:
                next_below = [lane_col(strips[k + 2], first + SUB + s) for s in range(SUB)]
            strip = jnp.where(inside, jnp.where(lane == sub + first, 1.0, 0.0), strip)
            recips = jnp.zeros(shape, jnp.float32)
            recip, scalars, rows = [], [], []
            yield
            for t in range(SUB):
                r = 1.0 / sub_row(cols[t], t)
                recips = jnp.where(sub == t, r, recips)
                masked = jnp.where(sub > t, cols[t], 0.0)
                factor = masked * r
                row = sub_row(strip, t)
                scalar = {}
                for s in range(t + 1, SUB):
                    scalar[s] = sub_row(cols[s], t)
                    cols[s] = cols[s] - ((masked * scalar[s]) * r if s == t + 1 else factor * scalar[s])
                if t < SUB - 1:
                    strip = strip - factor * row
                recip.append(r)
                scalars.append(scalar)
                rows.append(row)
                if next_cols is not None:
                    col = below[k + 1]
                    factor = col[t] * r
                    for s in range(t + 1, SUB):
                        col[s] = col[s] - factor * scalar[s]
                    across = [sub_row(col[t], s) for s in range(SUB)]
                    for s in range(SUB):
                        next_cols[s] = next_cols[s] - factor * across[s]
                    if next_below is not None:
                        col = below[k + 2]
                        factor = col[t] * r
                        for s in range(t + 1, SUB):
                            col[s] = col[s] - factor * scalar[s]
                        for s in range(SUB):
                            next_below[s] = next_below[s] - factor * across[s]
                yield
            for g in range(k + 1, end):
                col = below[g]
                done = (g == k + 1 and next_cols is not None) or (g == k + 2 and next_below is not None)
                rest = jnp.where(inside, 0.0, strips[g])
                for t in range(SUB):
                    factor = col[t] * recip[t]
                    if not done:
                        for s in range(t + 1, SUB):
                            col[s] = col[s] - factor * scalars[t][s]
                    rest = rest - factor * rows[t]
                strips[g] = rest
                yield
            strip = strip * (recips * lax.rsqrt(recips))
            out.append(jnp.where(lane < first + SUB, strip, 0.0))
            finished.append(jnp.where((lane < first + SUB) | (lane >= SUB * end), strip, 0.0))
        if end < groups:
            rows = jnp.concatenate(finished, axis=0)
            update = mm_tn(rows[:, SUB * end :], rows)
            cleared = (lane >= SUB * opening) & (lane < SUB * end)
            for g in range(end, groups):
                start = SUB * (g - end)
                strips[g] = jnp.where(cleared, 0.0, strips[g]) - update[start : start + SUB, :]
            yield
    return jnp.concatenate(out, axis=0)


def interleave(steps):
    results = [None] * len(steps)
    live = list(range(len(steps)))
    while live:
        for i in list(live):
            try:
                next(steps[i])
            except StopIteration as stop:
                results[i] = stop.value
                live.remove(i)
    return results


def rotate(gram_ref, work):
    lead_ref, trail_ref, first_ref, alone_ref, inv_ref = work

    def close_step():
        lead, trail, lead_inv = lead_ref[...], trail_ref[...], inv_ref[...]
        first = mm(lead_inv, lead)
        corner = mm_nt(mm_nt(trail, lead), lead_inv)
        rest = mm_nt(trail, trail) - mm_nt(corner, corner)
        return first, rest, trail - mm(corner, first)

    def both(iteration, carry):
        first, rest, remainder = close_step()
        lead = mm(first, gram_ref[...])
        lead_inv, trail_inv = interleave(
            [factor_steps(mm_nt(lead, lead), *PAIRED), factor_steps(rest, *PAIRED)]
        )
        lead_ref[...] = lead
        inv_ref[...] = lead_inv
        trail_ref[...] = mm(trail_inv, mm(remainder, gram_ref[...]))
        return carry

    def alone(end, carry):
        inv_ref[...] = interleave([factor_steps(alone_ref[...], *ALONE)])[0]

        @pl.when(end == 0)
        def _():
            lax.fori_loop(0, EIG_ITERS - 1, both, 0)
            first_ref[...], alone_ref[...], trail_ref[...] = close_step()

        return carry

    lead_ref[...] = gram_ref[:BLOCK]
    trail_ref[...] = gram_ref[BLOCK:]
    lead = lead_ref[...]
    alone_ref[...] = mm_nt(lead, lead)
    lax.fori_loop(0, 2, alone, 0)
    return first_ref[...], mm(inv_ref[...], trail_ref[...])


def work_refs():
    tall, square = pltpu.VMEM((BLOCK, 2 * BLOCK), jnp.float32), pltpu.VMEM((BLOCK, BLOCK), jnp.float32)
    return [tall, tall, tall, square, square]


def diagonal_mask(size):
    shape = (size, size)
    return lax.broadcasted_iota(jnp.int32, shape, 0) - lax.broadcasted_iota(jnp.int32, shape, 1)


def diagonal_row(square):
    size = square.shape[0]
    kept = jnp.where(diagonal_mask(size) == 0, square, 0.0)
    return jnp.broadcast_to(jnp.sum(kept, axis=0, keepdims=True), (SUB, size))


def pack(first, second):
    return jnp.where(diagonal_mask(BLOCK) <= 0, first, second)


def unpack(packed, row):
    below = diagonal_mask(BLOCK)
    turned = packed.T
    first = jnp.where(below <= 0, packed, turned)
    second = jnp.where(below > 0, packed, jnp.where(below < 0, turned, jnp.broadcast_to(row, packed.shape)))
    return first, second


def fill_gram(gram_ref, first, cross, second):
    gram_ref[:BLOCK, :BLOCK] = first
    gram_ref[:BLOCK, BLOCK:] = cross
    gram_ref[BLOCK:, :BLOCK] = cross.T
    gram_ref[BLOCK:, BLOCK:] = second


def first_round_kernel(parts_ref, out_ref, gram_ref, *work):
    first, second = unpack(parts_ref[:BLOCK], parts_ref[2 * BLOCK : 2 * BLOCK + 1])
    fill_gram(gram_ref, first, parts_ref[BLOCK : 2 * BLOCK], second)
    gram = gram_ref[...]
    first, second = rotate(gram_ref, work)
    out_ref[:BLOCK] = first
    out_ref[HALF_ROWS : HALF_ROWS + BLOCK] = second
    first = mm_nt(mm(first, gram), first)
    second = mm_nt(mm(second, gram), second)
    packed = pack(first, second)
    for i, (start, lanes) in enumerate(PACK_PLACES):
        out_ref[start : start + PACK, lanes : lanes + BLOCK] = packed[i * PACK : (i + 1) * PACK]
    out_ref[2 * HALF_ROWS :, :BLOCK] = diagonal_row(second)
    out_ref[2 * HALF_ROWS :, BLOCK:] = jnp.zeros((SUB, BLOCK), jnp.float32)


def slot_of(pairing, sweep, block, blocks):
    slot = 0
    for s in range(blocks):
        slot = slot + jnp.where(pairing[sweep, s] == block, s, 0)
    return slot


def part_copies(part, target, sem):
    copies = []
    start = 0
    for piece in part:
        rows = piece.shape[0]
        copies.append(pltpu.make_async_copy(piece, target.at[start : start + rows], sem))
        start += rows
    return copies


def grouped(refs, layout):
    refs = list(refs)
    parts = []
    for pieces in layout:
        parts.append(refs[:pieces])
        refs = refs[pieces:]
    return parts, refs


def second_round_kernel(blocks, layout, total_rows, pairing, ids, *refs):
    parts, (cross_ref, out_ref, turned, gram_ref, sems, *work) = grouped(refs, layout)
    owner = ids[2]
    order = 2 * BLOCK
    slots = [slot_of(pairing, 0, pairing[1, 2 * owner + side], blocks) for side in range(2)]
    for side in range(2):
        wanted = owner ^ (slots[side] // 2)
        for d, part in enumerate(parts):

            @pl.when(wanted == d)
            def _():
                for copy in part_copies(part, turned.at[side], sems.at[side]):
                    copy.start()

    for side in range(2):
        arrive(turned.at[side], sems.at[side])
    halves, owns = [], []
    for side in range(2):
        which = slots[side] % 2
        start = pl.multiple_of(which * HALF_ROWS, SUB)
        halves.append(turned[side, pl.ds(start, BLOCK), :])
        packed = jnp.concatenate(
            [turned[side, at : at + PACK, lanes : lanes + BLOCK] for at, lanes in PACK_PLACES], axis=0
        )
        pair = unpack(packed, turned[side, 2 * HALF_ROWS : 2 * HALF_ROWS + 1, :BLOCK])
        owns.append(jnp.where(which == 0, pair[0], pair[1]))
    cross = mm_nt(mm(halves[0], cross_ref[...]), halves[1])
    fill_gram(gram_ref, owns[0], cross, owns[1])
    gram = gram_ref[...]
    rotation = jnp.concatenate(rotate(gram_ref, work), axis=0)
    squares = mm_nt(mm(rotation, gram), rotation)
    kept = jnp.where(diagonal_mask(order) == 0, squares, 0.0)
    scale = jnp.sqrt(jnp.sum(kept, axis=1, keepdims=True) / total_rows + epsilon)
    out_ref[:order] = rotation / scale
    out_ref[order:] = jnp.sqrt(diagonal_row(squares) / total_rows + epsilon)


def fetch_block(parts, block, target, sem, place, slots):
    wanted = (block // slots) ^ place
    start = pl.multiple_of((block % slots) * BLOCK, BLOCK)
    for d, part in enumerate(parts):

        @pl.when(wanted == d)
        def _():
            pltpu.make_async_copy(part.at[:, pl.ds(start, BLOCK)], target, sem).start()


def arrive(target, sem):
    pltpu.make_async_copy(target, target, sem).wait()


def own_gram_kernel(slots, pairing, ids, *refs):
    *parts, own_ref, other_ref, held, sems = refs
    place, low = ids[0], ids[1]
    tasks = ((other_ref, 1 - low), (own_ref, low))
    for i, (_, s) in enumerate(tasks):
        for side in range(2):
            block = pairing[0, 2 * (place * (slots // 2) + s) + side]
            fetch_block(parts, block, held.at[2 * i + side], sems.at[2 * i + side], place, slots)
    for i, (out_ref, _) in enumerate(tasks):
        for side in range(2):
            arrive(held.at[2 * i + side], sems.at[2 * i + side])
        lead, trail = held[2 * i], held[2 * i + 1]
        second = mm_tn(trail, trail)
        out_ref[:BLOCK] = pack(mm_tn(lead, lead), second)
        out_ref[BLOCK : 2 * BLOCK] = mm_tn(lead, trail)
        out_ref[2 * BLOCK :] = diagonal_row(second)


def cross_gram_kernel(slots, blocks, pairing, ids, *refs):
    *parts, own_ref, other_ref, held, sems = refs
    place, low = ids[0], ids[1]
    tasks = ((other_ref, 1 - low), (own_ref, low))
    for i, (_, s) in enumerate(tasks):
        pair = place * (slots // 2) + s
        for side in range(2):
            source = slot_of(pairing, 0, pairing[1, 2 * pair + side], blocks) // 2
            at = 2 * i + side
            for j in range(2):
                fetch_block(
                    parts,
                    pairing[0, 2 * source + j],
                    held.at[at, :, j * BLOCK : (j + 1) * BLOCK],
                    sems.at[2 * at + j],
                    place,
                    slots,
                )
    for i, (out_ref, _) in enumerate(tasks):
        for at in (2 * i, 2 * i + 1):
            for j in range(2):
                arrive(held.at[at, :, j * BLOCK : (j + 1) * BLOCK], sems.at[2 * at + j])
        out_ref[...] = mm_tn(held[2 * i], held[2 * i + 1])


def first_turn_kernel(slots, places, layout, pairing, ids, *refs):
    parts, rest = refs[:places], refs[places:]
    turned_parts, (out_ref, held, turned, sems) = grouped(rest, layout)
    place, owner = ids[0], ids[2]
    blocks = slots * places
    copies = []
    for d, part in enumerate(turned_parts):
        copies += part_copies(part, turned.at[owner ^ d], sems.at[places + d])
    for d, part in enumerate(parts):
        for j in range(slots):
            copies.append(
                pltpu.make_async_copy(
                    part.at[:, j * BLOCK : (j + 1) * BLOCK], held.at[(place ^ d) * slots + j], sems.at[d]
                )
            )
    for copy in copies:
        copy.start()
    for d in range(len(turned_parts)):
        arrive(turned.at[0], sems.at[places + d])
    for d in range(places):
        arrive(held.at[:slots], sems.at[d])
    for j in range(slots):
        pair = slot_of(pairing, 1, place * slots + j, blocks) // 2
        for side in range(2):
            slot = slot_of(pairing, 0, pairing[1, 2 * pair + side], blocks)
            source = slot // 2
            half = turned[source, pl.ds(pl.multiple_of((slot % 2) * HALF_ROWS, SUB), BLOCK), :]
            joined = jnp.concatenate([held[pairing[0, 2 * source]], held[pairing[0, 2 * source + 1]]], axis=1)
            out_ref[j, :, side * BLOCK : (side + 1) * BLOCK] = mm_nt_three(joined, half)


def last_turn_kernel(slots, blocks, layout, pairing, ids, columns_ref, *refs):
    turned_parts, (left_ref, spec_ref, turned, sems) = grouped(refs, layout)
    place, owner = ids[0], ids[2]
    for d, part in enumerate(turned_parts):
        for copy in part_copies(part, turned.at[owner ^ d], sems.at[d]):
            copy.start()
    for d in range(len(turned_parts)):
        arrive(turned.at[0], sems.at[d])
    for j in range(slots):
        slot = slot_of(pairing, 1, place * slots + j, blocks)
        pair = slot // 2
        start = pl.multiple_of((slot % 2) * BLOCK, BLOCK)
        left_ref[:, j * BLOCK : (j + 1) * BLOCK] = mm_nt_three(
            columns_ref[j], turned[pair, pl.ds(start, BLOCK), :]
        )
        spec_ref[:, j * BLOCK : (j + 1) * BLOCK] = turned[pair, 2 * BLOCK : 2 * BLOCK + 1, pl.ds(start, BLOCK)]


def exchange(x, axis, bit):
    size = lax.axis_size(axis)
    return lax.ppermute(x, axis, [(i, i ^ bit) for i in range(size)])


def gather_pairwise(x):
    result = {0: x}
    bit = lax.axis_size("pair") // 2
    while bit:
        for d, part in list(result.items()):
            result[d ^ bit] = exchange(part, "pair", bit)
        bit //= 2
    return [result[d] for d in range(len(result))]


def gather_owners(x, cut, beside=None):
    far = lax.axis_size("pair") // 2
    across = exchange(x, "row", 1)
    over = exchange(x, "pair", far)
    if beside is not None:
        across, over, beside = lax.optimization_barrier((across, over, beside))
    lower = exchange(across[:cut], "pair", far)
    upper = exchange(over[cut:], "row", 1)
    result = {0: [x], 1: [across], 2 * far: [over], 2 * far + 1: [lower, upper]}
    bit = far // 2
    while bit:
        for d, part in list(result.items()):
            result[d ^ (2 * bit)] = [exchange(piece, "pair", bit) for piece in part]
        bit //= 2
    return [result[d] for d in range(len(result))], beside


def sum_rows(first, second):
    total = first[0] + exchange(first[1], "row", 1)
    total, second = lax.optimization_barrier((total, second))
    behind = (second[0], second[1], 1)
    bit = 2
    while bit < lax.axis_size("row"):
        trailing = behind[0] + exchange(behind[1], "row", behind[2])
        total = total + exchange(total, "row", bit)
        total, trailing = lax.optimization_barrier((total, trailing))
        behind = (trailing, trailing, bit)
        bit *= 2
    return total, behind[0] + exchange(behind[1], "row", behind[2])


vmem = pl.BlockSpec(memory_space=pltpu.VMEM)
smem = pl.BlockSpec(memory_space=pltpu.SMEM)
hbm = pl.BlockSpec(memory_space=pl.ANY)


def call(kernel, in_specs, out_shapes, scratch=(), name=None, flops=0):
    return pl.pallas_call(
        kernel,
        out_shape=[jax.ShapeDtypeStruct(s, jnp.float32) for s in out_shapes],
        in_specs=in_specs,
        out_specs=[vmem] * len(out_shapes),
        scratch_shapes=list(scratch),
        compiler_params=pltpu.CompilerParams(vmem_limit_bytes=VMEM_LIMIT),
        cost_estimate=pl.CostEstimate(flops=flops, bytes_accessed=1 << 20, transcendentals=0),
        name=name,
    )


def flat(parts):
    return [piece for part in parts for piece in part], tuple(len(part) for part in parts)


def shards(snapshots, pairing):
    rows_dev, cols_dev = snapshots.shape
    slots = cols_dev // BLOCK
    places = lax.axis_size("pair")
    blocks = places * slots
    total_rows = rows_dev * lax.axis_size("row")
    order = 2 * BLOCK
    place = lax.axis_index("pair")
    low = lax.axis_index("row") % 2
    ids = jnp.stack([place, low, place * 2 + low]).astype(jnp.int32)

    f32 = jnp.float32
    dma = pltpu.SemaphoreType.DMA
    square = (order, order)
    packed = (order + SUB, BLOCK)
    parts = gather_pairwise(snapshots)
    own_grams = call(
        functools.partial(own_gram_kernel, slots),
        [smem, smem] + [hbm] * places,
        [packed, packed],
        [pltpu.VMEM((4, rows_dev, BLOCK), f32), dma((4,))],
        "own_gram",
    )(pairing, ids, *parts)
    cross_grams = call(
        functools.partial(cross_gram_kernel, slots, blocks),
        [smem, smem] + [hbm] * places,
        [square, square],
        [pltpu.VMEM((4, rows_dev, order), f32), dma((8,))],
        "cross_gram",
        1 << 31,
    )(pairing, ids, *parts)
    own_gram, cross_gram = sum_rows(own_grams, cross_grams)

    chain = 1 << 34
    (turned,) = call(
        first_round_kernel, [vmem], [(STEP_ROWS, order)], [pltpu.VMEM(square, f32)] + work_refs(), "first_round", chain
    )(own_gram)
    turned, cross_gram = lax.optimization_barrier((turned, cross_gram))
    gathered, _ = gather_owners(turned, HALF_ROWS)
    turned_parts, layout = flat(gathered)
    (second,) = call(
        functools.partial(second_round_kernel, blocks, layout, total_rows),
        [smem, smem] + [hbm] * len(turned_parts) + [vmem],
        [(order + SUB, order)],
        [pltpu.VMEM((2, STEP_ROWS, order), f32), pltpu.VMEM(square, f32), dma((2,))] + work_refs(),
        "second_round",
        chain,
    )(pairing, ids, *turned_parts, cross_gram)
    parts, second = lax.optimization_barrier((parts, second))
    (columns,) = call(
        functools.partial(first_turn_kernel, slots, places, layout),
        [smem, smem] + [hbm] * (places + len(turned_parts)),
        [(slots, rows_dev, order)],
        [
            pltpu.VMEM((blocks, rows_dev, BLOCK), f32),
            pltpu.VMEM((len(gathered), STEP_ROWS, order), f32),
            dma((places + len(gathered),)),
        ],
        "first_turn",
        1 << 32,
    )(pairing, ids, *parts, *turned_parts)
    gathered, columns = gather_owners(second, BLOCK, columns)
    second_parts, layout = flat(gathered)
    left, spectrum = call(
        functools.partial(last_turn_kernel, slots, blocks, layout),
        [smem, smem, vmem] + [hbm] * len(second_parts),
        [(rows_dev, cols_dev), (1, cols_dev)],
        [
            pltpu.VMEM((len(gathered), order + SUB, order), f32),
            dma((len(gathered),)),
        ],
        "last_turn",
    )(pairing, ids, columns, *second_parts)
    return left, spectrum.reshape(cols_dev)


def solution(mesh):
    return jax.shard_map(
        shards,
        mesh=mesh,
        in_specs=(P("row", "pair"), P()),
        out_specs=(P("row", "pair"), P("pair")),
        check_vma=False,
    )
```

time: 1030 us -> 140 us (0.14)
  other arithmetic: 642 us -> 0.23 us
  waiting for transfers between devices: 250 us -> 56.4 us
  matrix products: 57.7 us -> 0 us
  Pallas kernels: 0 us -> 53.4 us
  local copies, waits for them, and re-layouts: 37.7 us -> 1.96 us
  starting transfers between devices: 0.42 us -> 26.7 us
  blocking collectives: 21.4 us -> 0 us
  between operations: 15.2 us -> 0.95 us
    another operation x63 -> x1, other arithmetic: 641 us -> 0.08 us  [shards(): ids = jnp.stack([place, low, place * 2 + low]).astype(jnp.int32)]
    psum x2 -> x0, waiting for transfers between devices: 145 us -> none  [whole_gram(): return lax.psum(partial_gram, 'row')]
    all_gather x3 -> x0, waiting for transfers between devices: 105 us -> none  [shards(): lax.all_gather(blocks, 'pair', axis=1, tiled=True)]
    ppermute x0 -> x27, waiting for transfers between devices: none -> 56.4 us  [exchange(): return lax.ppermute(x, axis, [(i, i ^ bit) for i in range(size)])]
    pallas_call x0 -> x6, Pallas kernels: none -> 53.4 us  [the longest x1 20.8 us: shards(): call(functools.partial(second_round_kernel, blocks, layout, total_rows),...]
    dot_general x19 -> x0, matrix products: 37.9 us -> none  [the longest x3 18.1 us: folding(): jnp.einsum('rnc,nk->rkc', segment, selection, precision=precise)]
    ppermute x0 -> x27, starting transfers between devices: none -> 26.7 us  [exchange(): return lax.ppermute(x, axis, [(i, i ^ bit) for i in range(size)])]
    another operation x55 -> x0, local copies, waits for them, and re-layouts: 24.8 us -> none  [the longest x43 24.6 us: orthogonal_factor(): jax.scipy.linalg.solve_triangular(factor_lower, jnp.swapaxes(image, -1, -...]
  transfers between devices with their start and end apart: 5 -> 27, of which waited for: 5 -> 17; matrix products, arithmetic and copies ran while one was open for 0% -> 0% of each run, Pallas kernels for 0% -> 19%
where the time goes in v2:
time: 140 us
  waiting for transfers between devices  56.4 us (40%)
  Pallas kernels  53.4 us (38%)
  starting transfers between devices  26.7 us (19%)
  local copies, waits for them, and re-layouts  1.96 us (1%)
    ppermute x27, waiting for transfers between devices, exchange(): return lax.ppermute(x, axis, [(i, i ^ bit) for i in range(size)])  56.4 us
    ppermute x27, starting transfers between devices, exchange(): return lax.ppermute(x, axis, [(i, i ^ bit) for i in range(size)])  26.7 us
    pallas_call x1, Pallas kernels, shards(): call(functools.partial(second_round_kernel, blocks, layout, total_rows),...  20.8 us
    pallas_call x1, Pallas kernels, shards(): call(first_round_kernel, [vmem], [(STEP_ROWS, order)], [pltpu.VMEM(square...  18.4 us
    pallas_call x1, Pallas kernels, shards(): call(functools.partial(first_turn_kernel, slots, places, layout), [smem,...  4.69 us
    pallas_call x1, Pallas kernels, shards(): call(functools.partial(last_turn_kernel, slots, blocks, layout), [smem, s...  3.52 us
    pallas_call x1, Pallas kernels, shards(): call(functools.partial(cross_gram_kernel, slots, blocks), [smem, smem] +...  3.44 us
  transfers between devices with their start and end apart: 27, of which 17 were waited for; matrix products, arithmetic and copies ran while one was open for 0% of the time, Pallas kernels for 19%

profile of v2, /device:TPU:0, one launch (start us, length us, event | category | flops | bytes accessed | tf_op | source)
XLA Modules:
  0.0 139.7 jit_solution(9374744854744780983)
XLA Ops:
  0.6 3.0 %collective-permute-start.1 = (f32[512,512]{1,0:T(8,128)}, f32[512,512]{1,0:T(8,128)S(1)}, u32[]{:S(2)}, u32[]{:S(2)}) collective-permute-start(f32[512,512]{1,0:T(8,128)} %refs_0_.4), channel_id=1, source_target_pairs={{0,2},{1,3},{2,0},{3,1},{4,6},{5,7},{6,4},{7,5},{8,10},{9,11},{10,... | collective-permute-start | bytes 3145736 | tf_op jit(solution)/shard_map/ppermute | solution.py:429
  3.7 23.4 %collective-permute-done.1.refs_2_ = f32[512,512]{1,0:T(8,128)S(1)} collective-permute-done((f32[512,512]{1,0:T(8,128)}, f32[512,512]{1,0:T(8,128)S(1)}, u32[]{:S(2)}, u32[]{:S(2)}) %collective-permute-start.1) | collective-permute-done | bytes 1048608 | tf_op jit(solution)/shard_map/ppermute | solution.py:429
  27.1 2.6 %collective-permute-done.2.refs_3_ = f32[512,512]{1,0:T(8,128)S(1)} collective-permute-done((f32[512,512]{1,0:T(8,128)S(1)}, f32[512,512]{1,0:T(8,128)S(1)}, u32[]{:S(2)}, u32[]{:S(2)}) %collective-permute-start.2) | collective-permute-done | bytes 1048608 | tf_op jit(solution)/shard_map/ppermute | solution.py:429
  31.6 2.5 %own_gram.1 = (f32[264,128]{1,0:T(8,128)S(1)}, f32[264,128]{1,0:T(8,128)S(1)}) custom-call(s32[2,16]{1,0:T(2,128)S(1)} %copy-done.2, s32[3]{0:T(128)S(1)} %pad_add_fusion.ids, f32[512,512]{1,0:T(8,128)S(1)} %copy-done, f32[512,512]{1,0:T(8,128)S(1)} %collective-permute-done.refs_1_, f32[512,512]{1,0:T(8,128)S(1)} %collective-permute-done.1.refs_2_, ...), custom_call_target="tpu_custom_call" | custom-call | bytes 1048576 | tf_op jit(solution)/shard_map/own_gram/pallas_call | solution.py:511
  34.2 1.8 %collective-permute-start.3 = (f32[264,128]{1,0:T(8,128)S(1)}, f32[264,128]{1,0:T(8,128)S(1)}, u32[]{:S(2)}, u32[]{:S(2)}) collective-permute-start(f32[264,128]{1,0:T(8,128)S(1)} %get-tuple-element.26), channel_id=1, source_target_pairs={{0,4},{4,0},{8,12},{12,8},{16,20},{20,16},{24,28},{28,24},{1,5},{5... | collective-permute-start | bytes 405512 | tf_op jit(solution)/shard_map/ppermute | solution.py:429
  35.9 3.4 %cross_gram.1 = (f32[256,256]{1,0:T(8,128)S(1)}, f32[256,256]{1,0:T(8,128)S(1)}) custom-call(s32[2,16]{1,0:T(2,128)S(1)} %copy-done.2, s32[3]{0:T(128)S(1)} %pad_add_fusion.ids, f32[512,512]{1,0:T(8,128)S(1)} %copy-done, f32[512,512]{1,0:T(8,128)S(1)} %collective-permute-done.refs_1_, f32[512,512]{1,0:T(8,128)S(1)} %collective-permute-done.1.refs_2_, ...), custom_call_target="tpu_custom_call" | custom-call | flops 2147483648 | bytes 1048576 | tf_op jit(solution)/shard_map/cross_gram/pallas_call | solution.py:518
  39.9 1.8 %collective-permute-start.5 = (f32[256,256]{1,0:T(8,128)S(1)}, f32[256,256]{1,0:T(8,128)S(1)}, u32[]{:S(2)}, u32[]{:S(2)}) collective-permute-start(f32[256,256]{1,0:T(8,128)S(1)} %get-tuple-element.31), channel_id=1, source_target_pairs={{0,4},{4,0},{8,12},{12,8},{16,20},{20,16},{24,28},{28,24},{1,5},{5... | collective-permute-start | bytes 786440 | tf_op jit(solution)/shard_map/ppermute | solution.py:429
  43.2 3.4 %collective-permute-done.4 = f32[264,128]{1,0:T(8,128)S(1)} collective-permute-done((f32[264,128]{1,0:T(8,128)S(1)}, f32[264,128]{1,0:T(8,128)S(1)}, u32[]{:S(2)}, u32[]{:S(2)}) %collective-permute-start.4) | collective-permute-done | bytes 135200 | tf_op jit(solution)/shard_map/ppermute | solution.py:429
  47.6 1.8 %collective-permute-start.7 = (f32[256,256]{1,0:T(8,128)S(1)}, f32[256,256]{1,0:T(8,128)S(1)}, u32[]{:S(2)}, u32[]{:S(2)}) collective-permute-start(f32[256,256]{1,0:T(8,128)S(1)} %add.29), channel_id=1, source_target_pairs={{0,8},{4,12},{8,0},{12,4},{16,24},{20,28},{24,16},{28,20},{1,9},{5... | collective-permute-start | bytes 786440 | tf_op jit(solution)/shard_map/ppermute | solution.py:429
  49.3 2.6 %collective-permute-start.6 = (f32[264,128]{1,0:T(8,128)S(1)}, f32[264,128]{1,0:T(8,128)S(1)}, u32[]{:S(2)}, u32[]{:S(2)}) collective-permute-start(f32[264,128]{1,0:T(8,128)S(1)} %add.28), channel_id=1, source_target_pairs={{0,16},{4,20},{8,24},{12,28},{16,0},{20,4},{24,8},{28,12},{1,17},{... | collective-permute-start | bytes 405512 | tf_op jit(solution)/shard_map/ppermute | solution.py:429
  51.9 4.8 %collective-permute-done.6 = f32[264,128]{1,0:T(8,128)S(1)} collective-permute-done((f32[264,128]{1,0:T(8,128)S(1)}, f32[264,128]{1,0:T(8,128)S(1)}, u32[]{:S(2)}, u32[]{:S(2)}) %collective-permute-start.6) | collective-permute-done | bytes 135200 | tf_op jit(solution)/shard_map/ppermute | solution.py:429
  57.3 2.6 %collective-permute-start.8 = (f32[256,256]{1,0:T(8,128)S(1)}, f32[256,256]{1,0:T(8,128)S(1)}, u32[]{:S(2)}, u32[]{:S(2)}) collective-permute-start(f32[256,256]{1,0:T(8,128)S(1)} %add.31), channel_id=1, source_target_pairs={{0,16},{4,20},{8,24},{12,28},{16,0},{20,4},{24,8},{28,12},{1,17},{... | collective-permute-start | bytes 786440 | tf_op jit(solution)/shard_map/ppermute | solution.py:429
  59.9 18.4 %first_round.1.refs_0_.refs_4_ = f32[328,256]{1,0:T(8,128)S(1)} custom-call(f32[264,128]{1,0:T(8,128)S(1)} %add.30.parts_ref), custom_call_target="tpu_custom_call" | custom-call | flops 17179869184 | bytes 1048576 | tf_op jit(solution)/shard_map/first_round/pallas_call | solution.py:529
  78.4 1.6 %collective-permute-start.12 = (f32[328,256]{1,0:T(8,128)S(1)}, f32[328,256]{1,0:T(8,128)S(1)}, u32[]{:S(2)}, u32[]{:S(2)}) collective-permute-start(f32[328,256]{1,0:T(8,128)S(1)} %first_round.1.refs_0_.refs_4_), channel_id=1, source_target_pairs={{0,2},{1,3},{2,0},{3,1},{4,6},{5,7},{6,4},{7,5},{8,10},{9,11},{10,... | collective-permute-start | bytes 1007624 | tf_op jit(solution)/shard_map/ppermute | solution.py:429
  81.4 4.5 %collective-permute-done.12.refs_4_.refs_8_ = f32[328,256]{1,0:T(8,128)S(1)} collective-permute-done((f32[328,256]{1,0:T(8,128)S(1)}, f32[328,256]{1,0:T(8,128)S(1)}, u32[]{:S(2)}, u32[]{:S(2)}) %collective-permute-start.12) | collective-permute-done | bytes 335904 | tf_op jit(solution)/shard_map/ppermute | solution.py:429
  89.7 1.7 %collective-permute-done.14.refs_6_.refs_10_ = f32[168,256]{1,0:T(8,128)S(1)} collective-permute-done((f32[168,256]{1,0:T(8,128)S(1)}, f32[168,256]{1,0:T(8,128)S(1)}, u32[]{:S(2)}, u32[]{:S(2)}) %collective-permute-start.14) | collective-permute-done | bytes 172064 | tf_op jit(solution)/shard_map/ppermute | solution.py:429
  91.5 4.2 %collective-permute-done.13.refs_5_.refs_9_ = f32[160,256]{1,0:T(8,128)S(1)} collective-permute-done((f32[160,256]{1,0:T(8,128)S(1)}, f32[160,256]{1,0:T(8,128)S(1)}, u32[]{:S(2)}, u32[]{:S(2)}) %collective-permute-start.13) | collective-permute-done | bytes 163872 | tf_op jit(solution)/shard_map/ppermute | solution.py:429
  97.1 20.8 %second_round.1.refs_0_ = f32[264,256]{1,0:T(8,128)S(1)} custom-call(s32[2,16]{1,0:T(2,128)S(1)} %copy-done.3, s32[3]{0:T(128)S(1)} %pad_add_fusion.ids, f32[328,256]{1,0:T(8,128)S(1)} %first_round.1.refs_0_.refs_4_, f32[328,256]{1,0:T(8,128)S(1)} %collective-permute-done.9.refs_1_.refs_5_, f32[328,256]{1,0:T(8,128)S(1)} %collective-permute-done.10.refs_2_.refs_6_, ...), custom_call_target="tpu_custom_call" | custom-call | flops 17179869184 | bytes 1048576 | tf_op jit(solution)/shard_map/second_round/pallas_call | solution.py:535
  119.8 4.7 %first_turn.1.columns_ref = f32[4,512,256]{2,1,0:T(8,128)S(1)} custom-call(s32[2,16]{1,0:T(2,128)S(1)} %copy-done.3, s32[3]{0:T(128)S(1)} %pad_add_fusion.ids, f32[512,512]{1,0:T(8,128)S(1)} %copy-done.1, f32[512,512]{1,0:T(8,128)S(1)} %collective-permute-done.refs_1_, f32[512,512]{1,0:T(8,128)S(1)} %collective-permute-done.1.refs_2_, ...), custom_call_target="tpu_custom_call" | custom-call | flops 4294967296 | bytes 1048576 | tf_op jit(solution)/shard_map/first_turn/pallas_call | solution.py:544
  124.5 1.6 %collective-permute-done.19.refs_4_ = f32[264,256]{1,0:T(8,128)S(1)} collective-permute-done((f32[264,256]{1,0:T(8,128)S(1)}, f32[264,256]{1,0:T(8,128)S(1)}, u32[]{:S(2)}, u32[]{:S(2)}) %collective-permute-start.19) | collective-permute-done | bytes 270368 | tf_op jit(solution)/shard_map/ppermute | solution.py:429
  126.5 1.6 %collective-permute-start.23 = (f32[136,256]{1,0:T(8,128)S(1)}, f32[136,256]{1,0:T(8,128)S(1)}, u32[]{:S(2)}, u32[]{:S(2)}) collective-permute-start(f32[136,256]{1,0:T(8,128)S(1)} %slice.15), channel_id=1, source_target_pairs={{0,4},{4,0},{8,12},{12,8},{16,20},{20,16},{24,28},{28,24},{1,5},{5... | collective-permute-start | bytes 417800 | tf_op jit(solution)/shard_map/ppermute | solution.py:429
  128.7 1.7 %collective-permute-start.22 = (f32[128,256]{1,0:T(8,128)S(1)}, f32[128,256]{1,0:T(8,128)S(1)}, u32[]{:S(2)}, u32[]{:S(2)}) collective-permute-start(f32[128,256]{1,0:T(8,128)S(1)} %slice.14), channel_id=1, source_target_pairs={{0,2},{1,3},{2,0},{3,1},{4,6},{5,7},{6,4},{7,5},{8,10},{9,11},{10,... | collective-permute-start | bytes 393224 | tf_op jit(solution)/shard_map/ppermute | solution.py:429
  131.6 3.0 %collective-permute-done.22.refs_5_ = f32[128,256]{1,0:T(8,128)S(1)} collective-permute-done((f32[128,256]{1,0:T(8,128)S(1)}, f32[128,256]{1,0:T(8,128)S(1)}, u32[]{:S(2)}, u32[]{:S(2)}) %collective-permute-start.22) | collective-permute-done | bytes 131104 | tf_op jit(solution)/shard_map/ppermute | solution.py:429
  136.0 3.5 %last_turn.1 = (f32[512,512]{1,0:T(8,128)}, f32[1,512]{1,0:T(1,128)}) custom-call(s32[2,16]{1,0:T(2,128)S(1)} %copy-done.3, s32[3]{0:T(128)S(1)} %pad_add_fusion.ids, f32[4,512,256]{2,1,0:T(8,128)S(1)} %first_turn.1.columns_ref, f32[264,256]{1,0:T(8,128)S(1)} %second_round.1.refs_0_, f32[264,256]{1,0:T(8,128)S(1)} %collective-permute-done.18.refs_1_, ...), custom_call_target="tpu_custom_call" | custom-call | bytes 1048576 | tf_op jit(solution)/shard_map/last_turn/pallas_call | solution.py:558
  (55 shorter events, 17.5 us)
Async XLA Ops:
  0.6 26.4 %collective-permute-start.1 = (f32[512,512]{1,0:T(8,128)}, f32[512,512]{1,0:T(8,128)S(1)}, u32[]{:S(2)}, u32[]{:S(2)}) collective-permute-start(f32[512,512]{1,0:T(8,128)} %refs_0_.4), channel_id=1, source_target_pairs={{0,2},{1,3},{2,0},{3,1},{4,6},{5,7},{6,4},{7,5},{8,10},{9,11},{10,... | collective-permute-start | bytes 3145736 | tf_op jit(solution)/shard_map/ppermute | solution.py:429
  3.7 23.5 %collective-permute-start = (f32[512,512]{1,0:T(8,128)}, f32[512,512]{1,0:T(8,128)S(1)}, u32[]{:S(2)}, u32[]{:S(2)}) collective-permute-start(f32[512,512]{1,0:T(8,128)} %refs_0_.4), channel_id=1, source_target_pairs={{0,1},{1,0},{2,3},{3,2},{4,5},{5,4},{6,7},{7,6},{8,9},{9,8},{10,11... | collective-permute-start | bytes 3145736 | tf_op jit(solution)/shard_map/ppermute | solution.py:429
  34.2 5.7 %collective-permute-start.3 = (f32[264,128]{1,0:T(8,128)S(1)}, f32[264,128]{1,0:T(8,128)S(1)}, u32[]{:S(2)}, u32[]{:S(2)}) collective-permute-start(f32[264,128]{1,0:T(8,128)S(1)} %get-tuple-element.26), channel_id=1, source_target_pairs={{0,4},{4,0},{8,12},{12,8},{16,20},{20,16},{24,28},{28,24},{1,5},{5... | collective-permute-start | bytes 405512 | tf_op jit(solution)/shard_map/ppermute | solution.py:429
  39.9 7.7 %collective-permute-start.5 = (f32[256,256]{1,0:T(8,128)S(1)}, f32[256,256]{1,0:T(8,128)S(1)}, u32[]{:S(2)}, u32[]{:S(2)}) collective-permute-start(f32[256,256]{1,0:T(8,128)S(1)} %get-tuple-element.31), channel_id=1, source_target_pairs={{0,4},{4,0},{8,12},{12,8},{16,20},{20,16},{24,28},{28,24},{1,5},{5... | collective-permute-start | bytes 786440 | tf_op jit(solution)/shard_map/ppermute | solution.py:429
  41.6 5.0 %collective-permute-start.4 = (f32[264,128]{1,0:T(8,128)S(1)}, f32[264,128]{1,0:T(8,128)S(1)}, u32[]{:S(2)}, u32[]{:S(2)}) collective-permute-start(f32[264,128]{1,0:T(8,128)S(1)} %add.27), channel_id=1, source_target_pairs={{0,8},{4,12},{8,0},{12,4},{16,24},{20,28},{24,16},{28,20},{1,9},{5... | collective-permute-start | bytes 405512 | tf_op jit(solution)/shard_map/ppermute | solution.py:429
  47.6 9.7 %collective-permute-start.7 = (f32[256,256]{1,0:T(8,128)S(1)}, f32[256,256]{1,0:T(8,128)S(1)}, u32[]{:S(2)}, u32[]{:S(2)}) collective-permute-start(f32[256,256]{1,0:T(8,128)S(1)} %add.29), channel_id=1, source_target_pairs={{0,8},{4,12},{8,0},{12,4},{16,24},{20,28},{24,16},{28,20},{1,9},{5... | collective-permute-start | bytes 786440 | tf_op jit(solution)/shard_map/ppermute | solution.py:429
  49.3 7.4 %collective-permute-start.6 = (f32[264,128]{1,0:T(8,128)S(1)}, f32[264,128]{1,0:T(8,128)S(1)}, u32[]{:S(2)}, u32[]{:S(2)}) collective-permute-start(f32[264,128]{1,0:T(8,128)S(1)} %add.28), channel_id=1, source_target_pairs={{0,16},{4,20},{8,24},{12,28},{16,0},{20,4},{24,8},{28,12},{1,17},{... | collective-permute-start | bytes 405512 | tf_op jit(solution)/shard_map/ppermute | solution.py:429
  57.3 21.0 %collective-permute-start.8 = (f32[256,256]{1,0:T(8,128)S(1)}, f32[256,256]{1,0:T(8,128)S(1)}, u32[]{:S(2)}, u32[]{:S(2)}) collective-permute-start(f32[256,256]{1,0:T(8,128)S(1)} %add.31), channel_id=1, source_target_pairs={{0,16},{4,20},{8,24},{12,28},{16,0},{20,4},{24,8},{28,12},{1,17},{... | collective-permute-start | bytes 786440 | tf_op jit(solution)/shard_map/ppermute | solution.py:429
  78.4 7.6 %collective-permute-start.12 = (f32[328,256]{1,0:T(8,128)S(1)}, f32[328,256]{1,0:T(8,128)S(1)}, u32[]{:S(2)}, u32[]{:S(2)}) collective-permute-start(f32[328,256]{1,0:T(8,128)S(1)} %first_round.1.refs_0_.refs_4_), channel_id=1, source_target_pairs={{0,2},{1,3},{2,0},{3,1},{4,6},{5,7},{6,4},{7,5},{8,10},{9,11},{10,... | collective-permute-start | bytes 1007624 | tf_op jit(solution)/shard_map/ppermute | solution.py:429
  80.0 9.0 %collective-permute-start.9 = (f32[328,256]{1,0:T(8,128)S(1)}, f32[328,256]{1,0:T(8,128)S(1)}, u32[]{:S(2)}, u32[]{:S(2)}) collective-permute-start(f32[328,256]{1,0:T(8,128)S(1)} %first_round.1.refs_0_.refs_4_), channel_id=1, source_target_pairs={{0,4},{4,0},{8,12},{12,8},{16,20},{20,16},{24,28},{28,24},{1,5},{5... | collective-permute-start | bytes 1007624 | tf_op jit(solution)/shard_map/ppermute | solution.py:429
  86.0 5.5 %collective-permute-start.14 = (f32[168,256]{1,0:T(8,128)S(1)}, f32[168,256]{1,0:T(8,128)S(1)}, u32[]{:S(2)}, u32[]{:S(2)}) collective-permute-start(f32[168,256]{1,0:T(8,128)S(1)} %slice.17), channel_id=1, source_target_pairs={{0,4},{4,0},{8,12},{12,8},{16,20},{20,16},{24,28},{28,24},{1,5},{5... | collective-permute-start | bytes 516104 | tf_op jit(solution)/shard_map/ppermute | solution.py:429
  87.5 8.1 %collective-permute-start.10 = (f32[328,256]{1,0:T(8,128)S(1)}, f32[328,256]{1,0:T(8,128)S(1)}, u32[]{:S(2)}, u32[]{:S(2)}) collective-permute-start(f32[328,256]{1,0:T(8,128)S(1)} %first_round.1.refs_0_.refs_4_), channel_id=1, source_target_pairs={{0,1},{1,0},{2,3},{3,2},{4,5},{5,4},{6,7},{7,6},{8,9},{9,8},{10,11... | collective-permute-start | bytes 1007624 | tf_op jit(solution)/shard_map/ppermute | solution.py:429
  87.5 9.5 %collective-permute-start.15 = (f32[328,256]{1,0:T(8,128)S(1)}, f32[328,256]{1,0:T(8,128)S(1)}, u32[]{:S(2)}, u32[]{:S(2)}) collective-permute-start(f32[328,256]{1,0:T(8,128)S(1)} %collective-permute-done.12.refs_4_.refs_8_), channel_id=1, source_target_pairs={{0,1},{1,0},{2,3},{3,2},{4,5},{5,4},{6,7},{7,6},{8,9},{9,8},{10,11... | collective-permute-start | bytes 1007624 | tf_op jit(solution)/shard_map/ppermute | solution.py:429
  89.0 8.1 %collective-permute-start.11 = (f32[328,256]{1,0:T(8,128)S(1)}, f32[328,256]{1,0:T(8,128)S(1)}, u32[]{:S(2)}, u32[]{:S(2)}) collective-permute-start(f32[328,256]{1,0:T(8,128)S(1)} %collective-permute-done.9.refs_1_.refs_5_), channel_id=1, source_target_pairs={{0,1},{1,0},{2,3},{3,2},{4,5},{5,4},{6,7},{7,6},{8,9},{9,8},{10,11... | collective-permute-start | bytes 1007624 | tf_op jit(solution)/shard_map/ppermute | solution.py:429
  89.0 6.7 %collective-permute-start.13 = (f32[160,256]{1,0:T(8,128)S(1)}, f32[160,256]{1,0:T(8,128)S(1)}, u32[]{:S(2)}, u32[]{:S(2)}) collective-permute-start(f32[160,256]{1,0:T(8,128)S(1)} %slice.16), channel_id=1, source_target_pairs={{0,2},{1,3},{2,0},{3,1},{4,6},{5,7},{6,4},{7,5},{8,10},{9,11},{10,... | collective-permute-start | bytes 491528 | tf_op jit(solution)/shard_map/ppermute | solution.py:429
  91.5 5.6 %collective-permute-start.17 = (f32[168,256]{1,0:T(8,128)S(1)}, f32[168,256]{1,0:T(8,128)S(1)}, u32[]{:S(2)}, u32[]{:S(2)}) collective-permute-start(f32[168,256]{1,0:T(8,128)S(1)} %collective-permute-done.14.refs_6_.refs_10_), channel_id=1, source_target_pairs={{0,1},{1,0},{2,3},{3,2},{4,5},{5,4},{6,7},{7,6},{8,9},{9,8},{10,11... | collective-permute-start | bytes 516104 | tf_op jit(solution)/shard_map/ppermute | solution.py:429
  117.9 8.2 %collective-permute-start.19 = (f32[264,256]{1,0:T(8,128)S(1)}, f32[264,256]{1,0:T(8,128)S(1)}, u32[]{:S(2)}, u32[]{:S(2)}) collective-permute-start(f32[264,256]{1,0:T(8,128)S(1)} %second_round.1.refs_0_), channel_id=1, source_target_pairs={{0,2},{1,3},{2,0},{3,1},{4,6},{5,7},{6,4},{7,5},{8,10},{9,11},{10,... | collective-permute-start | bytes 811016 | tf_op jit(solution)/shard_map/ppermute | solution.py:429
  118.3 8.2 %collective-permute-start.18 = (f32[264,256]{1,0:T(8,128)S(1)}, f32[264,256]{1,0:T(8,128)S(1)}, u32[]{:S(2)}, u32[]{:S(2)}) collective-permute-start(f32[264,256]{1,0:T(8,128)S(1)} %second_round.1.refs_0_), channel_id=1, source_target_pairs={{0,4},{4,0},{8,12},{12,8},{16,20},{20,16},{24,28},{28,24},{1,5},{5... | collective-permute-start | bytes 811016 | tf_op jit(solution)/shard_map/ppermute | solution.py:429
  126.5 5.1 %collective-permute-start.23 = (f32[136,256]{1,0:T(8,128)S(1)}, f32[136,256]{1,0:T(8,128)S(1)}, u32[]{:S(2)}, u32[]{:S(2)}) collective-permute-start(f32[136,256]{1,0:T(8,128)S(1)} %slice.15), channel_id=1, source_target_pairs={{0,4},{4,0},{8,12},{12,8},{16,20},{20,16},{24,28},{28,24},{1,5},{5... | collective-permute-start | bytes 417800 | tf_op jit(solution)/shard_map/ppermute | solution.py:429
  128.1 6.5 %collective-permute-start.20 = (f32[264,256]{1,0:T(8,128)S(1)}, f32[264,256]{1,0:T(8,128)S(1)}, u32[]{:S(2)}, u32[]{:S(2)}) collective-permute-start(f32[264,256]{1,0:T(8,128)S(1)} %second_round.1.refs_0_), channel_id=1, source_target_pairs={{0,1},{1,0},{2,3},{3,2},{4,5},{5,4},{6,7},{7,6},{8,9},{9,8},{10,11... | collective-permute-start | bytes 811016 | tf_op jit(solution)/shard_map/ppermute | solution.py:429
  128.1 7.9 %collective-permute-start.21 = (f32[264,256]{1,0:T(8,128)S(1)}, f32[264,256]{1,0:T(8,128)S(1)}, u32[]{:S(2)}, u32[]{:S(2)}) collective-permute-start(f32[264,256]{1,0:T(8,128)S(1)} %collective-permute-done.18.refs_1_), channel_id=1, source_target_pairs={{0,1},{1,0},{2,3},{3,2},{4,5},{5,4},{6,7},{7,6},{8,9},{9,8},{10,11... | collective-permute-start | bytes 811016 | tf_op jit(solution)/shard_map/ppermute | solution.py:429
  128.7 7.3 %collective-permute-start.24 = (f32[264,256]{1,0:T(8,128)S(1)}, f32[264,256]{1,0:T(8,128)S(1)}, u32[]{:S(2)}, u32[]{:S(2)}) collective-permute-start(f32[264,256]{1,0:T(8,128)S(1)} %collective-permute-done.19.refs_4_), channel_id=1, source_target_pairs={{0,1},{1,0},{2,3},{3,2},{4,5},{5,4},{6,7},{7,6},{8,9},{9,8},{10,11... | collective-permute-start | bytes 811016 | tf_op jit(solution)/shard_map/ppermute | solution.py:429
  128.7 6.0 %collective-permute-start.22 = (f32[128,256]{1,0:T(8,128)S(1)}, f32[128,256]{1,0:T(8,128)S(1)}, u32[]{:S(2)}, u32[]{:S(2)}) collective-permute-start(f32[128,256]{1,0:T(8,128)S(1)} %slice.14), channel_id=1, source_target_pairs={{0,2},{1,3},{2,0},{3,1},{4,6},{5,7},{6,4},{7,5},{8,10},{9,11},{10,... | collective-permute-start | bytes 393224 | tf_op jit(solution)/shard_map/ppermute | solution.py:429
  131.6 4.4 %collective-permute-start.26 = (f32[136,256]{1,0:T(8,128)S(1)}, f32[136,256]{1,0:T(8,128)S(1)}, u32[]{:S(2)}, u32[]{:S(2)}) collective-permute-start(f32[136,256]{1,0:T(8,128)S(1)} %collective-permute-done.23.refs_6_), channel_id=1, source_target_pairs={{0,1},{1,0},{2,3},{3,2},{4,5},{5,4},{6,7},{7,6},{8,9},{9,8},{10,11... | collective-permute-start | bytes 417800 | tf_op jit(solution)/shard_map/ppermute | solution.py:429
  (7 other events, 77.9 us)

commit v3 on v2

--- a/solution.py
+++ b/solution.py
@@ -19,8 +19,6 @@
 HALF_ROWS = BLOCK + PACK
 STEP_ROWS = 2 * HALF_ROWS + SUB
 PACK_PLACES = ((BLOCK, 0), (BLOCK, BLOCK), (HALF_ROWS + BLOCK, 0), (HALF_ROWS + BLOCK, BLOCK))
-ALONE = (64, 2)
-PAIRED = (32, 1)
 
 
 def mm(a, b):
@@ -62,8 +60,8 @@
     return jnp.broadcast_to(v[:, l : l + 1], v.shape)
 
 
-def factor_steps(matrix, panel, ahead):
-    groups, strips_panel = BLOCK // SUB, panel // SUB
+def inverse_factor(matrix):
+    groups, strips_panel = BLOCK // SUB, BLOCK // SUB // 2
     shape = (SUB, BLOCK)
     sub = lax.broadcasted_iota(jnp.int32, shape, 0)
     lane = lax.broadcasted_iota(jnp.int32, shape, 1)
@@ -87,14 +85,13 @@
                 else:
                     below[g] = [lane_col(strips[g], first + s) for s in range(SUB)]
             next_cols = next_below = None
-            if ahead >= 1 and k + 1 < end:
+            if k + 1 < end:
                 next_cols = [lane_col(strips[k + 1], first + SUB + s) for s in range(SUB)]
-            if ahead >= 2 and k + 2 < end:
+            if k + 2 < end:
                 next_below = [lane_col(strips[k + 2], first + SUB + s) for s in range(SUB)]
             strip = jnp.where(inside, jnp.where(lane == sub + first, 1.0, 0.0), strip)
             recips = jnp.zeros(shape, jnp.float32)
             recip, scalars, rows = [], [], []
-            yield
             for t in range(SUB):
                 r = 1.0 / sub_row(cols[t], t)
                 recips = jnp.where(sub == t, r, recips)
@@ -125,7 +122,6 @@
                             col[s] = col[s] - factor * scalar[s]
                         for s in range(SUB):
                             next_below[s] = next_below[s] - factor * across[s]
-                yield
             for g in range(k + 1, end):
                 col = below[g]
                 done = (g == k + 1 and next_cols is not None) or (g == k + 2 and next_below is not None)
@@ -137,7 +133,6 @@
                             col[s] = col[s] - factor * scalars[t][s]
                     rest = rest - factor * rows[t]
                 strips[g] = rest
-                yield
             strip = strip * (recips * lax.rsqrt(recips))
             out.append(jnp.where(lane < first + SUB, strip, 0.0))
             finished.append(jnp.where((lane < first + SUB) | (lane >= SUB * end), strip, 0.0))
@@ -148,25 +143,98 @@
             for g in range(end, groups):
                 start = SUB * (g - end)
                 strips[g] = jnp.where(cleared, 0.0, strips[g]) - update[start : start + SUB, :]
-            yield
     return jnp.concatenate(out, axis=0)
 
 
-def interleave(steps):
-    results = [None] * len(steps)
-    live = list(range(len(steps)))
-    while live:
-        for i in list(live):
-            try:
-                next(steps[i])
-            except StopIteration as stop:
-                results[i] = stop.value
-                live.remove(i)
-    return results
+def paired_factors(first, second):
+    groups, half = BLOCK // SUB, BLOCK // 2
+    panel = groups // 2
+    shape = (SUB, BLOCK)
+    sub = lax.broadcasted_iota(jnp.int32, shape, 0)
+    lane = lax.broadcasted_iota(jnp.int32, shape, 1)
+    low = lane < half
+    base = jnp.where(low, 0, half)
+    lane = lane - base
+    left = lax.broadcasted_iota(jnp.int32, (BLOCK, BLOCK), 1) < half
+
+    def regroup(x, y):
+        return [jnp.where(left, x, pltpu.roll(y, half, 1)), jnp.where(left, pltpu.roll(x, half, 1), y)]
+
+    def column(v, l):
+        return jnp.take_along_axis(v, base + l, axis=1)
+
+    packed = regroup(first, second)
+    strips = [[side[SUB * g : SUB * (g + 1)] for side in packed] for g in range(groups)]
+    out = []
+    for part in range(2):
+        opening, end = panel * part, panel * (part + 1)
+        next_cols = None
+        finished = []
+        for k in range(opening, end):
+            at = SUB * (k - opening)
+            inside = (lane >= at) & (lane < at + SUB)
+            strip = list(strips[k])
+            cols = next_cols
+            if cols is None:
+                cols = [column(strip[part], at + s) for s in range(SUB)]
+            below = {g: [column(strips[g][part], at + s) for s in range(SUB)] for g in range(k + 1, end)}
+            next_cols = None
+            if k + 1 < end:
+                next_cols = [column(strips[k + 1][part], at + SUB + s) for s in range(SUB)]
+            strip[part] = jnp.where(inside, jnp.where(lane == sub + at, 1.0, 0.0), strip[part])
+            recips = jnp.zeros(shape, jnp.float32)
+            recip, scalars, rows = [], [], []
+            for t in range(SUB):
+                r = 1.0 / sub_row(cols[t], t)
+                recips = jnp.where(sub == t, r, recips)
+                masked = jnp.where(sub > t, cols[t], 0.0)
+                factor = masked * r
+                row = [sub_row(side, t) for side in strip]
+                scalar = {}
+                for s in range(t + 1, SUB):
+                    scalar[s] = sub_row(cols[s], t)
+                    cols[s] = cols[s] - ((masked * scalar[s]) * r if s == t + 1 else factor * scalar[s])
+                if t < SUB - 1:
+                    strip = [side - factor * line for side, line in zip(strip, row)]
+                recip.append(r)
+                scalars.append(scalar)
+                rows.append(row)
+                if next_cols is not None:
+                    col = below[k + 1]
+                    factor = col[t] * r
+                    for s in range(t + 1, SUB):
+                        col[s] = col[s] - factor * scalar[s]
+                    for s in range(SUB):
+                        next_cols[s] = next_cols[s] - factor * sub_row(col[t], s)
+            for g in range(k + 1, end):
+                col = below[g]
+                rest = list(strips[g])
+                rest[part] = jnp.where(inside, 0.0, rest[part])
+                for t in range(SUB):
+                    factor = col[t] * recip[t]
+                    if g > k + 1:
+                        for s in range(t + 1, SUB):
+                            col[s] = col[s] - factor * scalars[t][s]
+                    rest = [side - factor * line for side, line in zip(rest, rows[t])]
+                strips[g] = rest
+            scale = recips * lax.rsqrt(recips)
+            strip = [side * scale for side in strip]
+            kept = jnp.where(lane < at + SUB, strip[part], 0.0)
+            out.append([kept, jnp.zeros(shape, jnp.float32)] if part == 0 else [strip[0], kept])
+            finished.append([kept, strip[1]])
+        if part == 0:
+            rows = [jnp.concatenate([strip[i] for strip in finished], axis=0) for i in range(2)]
+            for i in range(2):
+                update = mm_tn(rows[1], rows[i])
+                for g in range(end, groups):
+                    start = SUB * (g - end)
+                    change = jnp.where(low, update[start : start + SUB], update[half + start : half + start + SUB])
+                    strips[g][i] = strips[g][i] - change if i == 1 else -change
+    return regroup(*[jnp.concatenate([strip[i] for strip in out], axis=0) for i in range(2)])
 
 
 def rotate(gram_ref, work):
-    lead_ref, trail_ref, first_ref, alone_ref, inv_ref = work
+    lead_ref, trail_ref, first_ref, image_ref, beside_ref, alone_ref, inv_ref = work
 
     def close_step():
         lead, trail, lead_inv = lead_ref[...], trail_ref[...], inv_ref[...]
@@ -177,17 +245,19 @@
 
     def both(iteration, carry):
         first, rest, remainder = close_step()
-        lead = mm(first, gram_ref[...])
-        lead_inv, trail_inv = interleave(
-            [factor_steps(mm_nt(lead, lead), *PAIRED), factor_steps(rest, *PAIRED)]
-        )
+        gram = gram_ref[...]
+        lead = mm(first, gram)
+        lead_inv, trail_inv = paired_factors(mm_nt(lead, lead), rest)
         lead_ref[...] = lead
         inv_ref[...] = lead_inv
-        trail_ref[...] = mm(trail_inv, mm(remainder, gram_ref[...]))
+        trail_ref[...] = mm(trail_inv, mm(remainder, gram))
         return carry
 
     def alone(end, carry):
-        inv_ref[...] = interleave([factor_steps(alone_ref[...], *ALONE)])[0]
+        gram = gram_ref[...]
+        inv_ref[...] = inverse_factor(alone_ref[...])
+        image_ref[...] = mm(first_ref[...], gram)
+        beside_ref[...] = mm(trail_ref[...], gram)
 
         @pl.when(end == 0)
         def _():
@@ -196,17 +266,19 @@
 
         return carry
 
-    lead_ref[...] = gram_ref[:BLOCK]
+    lead = gram_ref[:BLOCK]
+    lead_ref[...] = lead
     trail_ref[...] = gram_ref[BLOCK:]
-    lead = lead_ref[...]
+    first_ref[...] = lead
     alone_ref[...] = mm_nt(lead, lead)
     lax.fori_loop(0, 2, alone, 0)
-    return first_ref[...], mm(inv_ref[...], trail_ref[...])
+    inv = inv_ref[...]
+    return first_ref[...], image_ref[...], mm(inv, trail_ref[...]), mm(inv, beside_ref[...])
 
 
 def work_refs():
     tall, square = pltpu.VMEM((BLOCK, 2 * BLOCK), jnp.float32), pltpu.VMEM((BLOCK, BLOCK), jnp.float32)
-    return [tall, tall, tall, square, square]
+    return [tall, tall, tall, tall, tall, square, square]
 
 
 def diagonal_mask(size):
@@ -242,12 +314,11 @@
 def first_round_kernel(parts_ref, out_ref, gram_ref, *work):
     first, second = unpack(parts_ref[:BLOCK], parts_ref[2 * BLOCK : 2 * BLOCK + 1])
     fill_gram(gram_ref, first, parts_ref[BLOCK : 2 * BLOCK], second)
-    gram = gram_ref[...]
-    first, second = rotate(gram_ref, work)
+    first, first_image, second, second_image = rotate(gram_ref, work)
     out_ref[:BLOCK] = first
     out_ref[HALF_ROWS : HALF_ROWS + BLOCK] = second
-    first = mm_nt(mm(first, gram), first)
-    second = mm_nt(mm(second, gram), second)
+    first = mm_nt(first_image, first)
+    second = mm_nt(second_image, second)
     packed = pack(first, second)
     for i, (start, lanes) in enumerate(PACK_PLACES):
         out_ref[start : start + PACK, lanes : lanes + BLOCK] = packed[i * PACK : (i + 1) * PACK]
@@ -282,7 +353,7 @@
 
 
 def second_round_kernel(blocks, layout, total_rows, pairing, ids, *refs):
-    parts, (cross_ref, out_ref, turned, gram_ref, sems, *work) = grouped(refs, layout)
+    parts, (kept_ref, other_ref, out_ref, turned, gram_ref, sems, *work) = grouped(refs, layout)
     owner = ids[2]
     order = 2 * BLOCK
     slots = [slot_of(pairing, 0, pairing[1, 2 * owner + side], blocks) for side in range(2)]
@@ -307,15 +378,17 @@
         )
         pair = unpack(packed, turned[side, 2 * HALF_ROWS : 2 * HALF_ROWS + 1, :BLOCK])
         owns.append(jnp.where(which == 0, pair[0], pair[1]))
-    cross = mm_nt(mm(halves[0], cross_ref[...]), halves[1])
+    kept, other = kept_ref[...], other_ref[...]
+    top = jnp.where(ids[3] == 0, kept, other)
+    bottom = jnp.where(ids[3] == 0, other, kept)
+    cross = mm_nt(mm(halves[0], jnp.concatenate([top, bottom], axis=0)), halves[1])
     fill_gram(gram_ref, owns[0], cross, owns[1])
-    gram = gram_ref[...]
-    rotation = jnp.concatenate(rotate(gram_ref, work), axis=0)
-    squares = mm_nt(mm(rotation, gram), rotation)
-    kept = jnp.where(diagonal_mask(order) == 0, squares, 0.0)
-    scale = jnp.sqrt(jnp.sum(kept, axis=1, keepdims=True) / total_rows + epsilon)
-    out_ref[:order] = rotation / scale
-    out_ref[order:] = jnp.sqrt(diagonal_row(squares) / total_rows + epsilon)
+    first, first_image, second, second_image = rotate(gram_ref, work)
+    for i, (half, image) in enumerate(((first, first_image), (second, second_image))):
+        lanes = slice(i * BLOCK, (i + 1) * BLOCK)
+        spectrum = jnp.sqrt(jnp.sum(half * image, axis=1, keepdims=True) / total_rows + epsilon)
+        out_ref[lanes] = half / spectrum
+        out_ref[order:, lanes] = diagonal_row(jnp.broadcast_to(spectrum, (BLOCK, BLOCK)))
 
 
 def fetch_block(parts, block, target, sem, place, slots):
@@ -372,7 +445,9 @@
         for at in (2 * i, 2 * i + 1):
             for j in range(2):
                 arrive(held.at[at, :, j * BLOCK : (j + 1) * BLOCK], sems.at[2 * at + j])
-        out_ref[...] = mm_tn(held[2 * i], held[2 * i + 1])
+        for j in range(2):
+            start = pl.multiple_of((j ^ ids[3]) * BLOCK, BLOCK)
+            out_ref[pl.ds(start, BLOCK)] = mm_tn(held[2 * i, :, j * BLOCK : (j + 1) * BLOCK], held[2 * i + 1])
 
 
 def first_turn_kernel(slots, places, layout, pairing, ids, *refs):
@@ -439,35 +514,49 @@
     return [result[d] for d in range(len(result))]
 
 
-def gather_owners(x, cut, beside=None):
+def gather_owners(x, cut, beside=None, second=None):
     far = lax.axis_size("pair") // 2
     across = exchange(x, "row", 1)
     over = exchange(x, "pair", far)
-    if beside is not None:
-        across, over, beside = lax.optimization_barrier((across, over, beside))
-    lower = exchange(across[:cut], "pair", far)
-    upper = exchange(over[cut:], "row", 1)
-    result = {0: [x], 1: [across], 2 * far: [over], 2 * far + 1: [lower, upper]}
+    result = {0: [x]}
     bit = far // 2
     while bit:
         for d, part in list(result.items()):
             result[d ^ (2 * bit)] = [exchange(piece, "pair", bit) for piece in part]
         bit //= 2
+    if beside is None:
+        across, over, result = lax.optimization_barrier((across, over, result))
+    else:
+        across, over, result, beside = lax.optimization_barrier((across, over, result, beside))
+    lower = exchange(across[:cut], "pair", far)
+    upper = exchange(over[cut:], "row", 1)
+    if second is not None:
+        beside = (beside, second(beside))
+        lower, upper, beside = lax.optimization_barrier((lower, upper, beside))
+    later = {1: [across], 2 * far: [over], 2 * far + 1: [lower, upper]}
+    bit = far // 2
+    while bit:
+        for d, part in list(later.items()):
+            later[d ^ (2 * bit)] = [exchange(piece, "pair", bit) for piece in part]
+        bit //= 2
+    result.update(later)
     return [result[d] for d in range(len(result))], beside
 
 
+def add_across(x, bit):
+    return x + exchange(x, "row", bit)
+
+
 def sum_rows(first, second):
+    rows = lax.axis_size("row")
     total = first[0] + exchange(first[1], "row", 1)
-    total, second = lax.optimization_barrier((total, second))
-    behind = (second[0], second[1], 1)
     bit = 2
-    while bit < lax.axis_size("row"):
-        trailing = behind[0] + exchange(behind[1], "row", behind[2])
-        total = total + exchange(total, "row", bit)
-        total, trailing = lax.optimization_barrier((total, trailing))
-        behind = (trailing, trailing, bit)
+    while bit < rows:
+        if 2 * bit >= rows:
+            total, second = lax.optimization_barrier((total, second))
+        total = add_across(total, bit)
         bit *= 2
-    return total, behind[0] + exchange(behind[1], "row", behind[2])
+    return total, second[0] + exchange(second[1], "row", 1)
 
 
 vmem = pl.BlockSpec(memory_space=pltpu.VMEM)
@@ -501,7 +590,8 @@
     order = 2 * BLOCK
     place = lax.axis_index("pair")
     low = lax.axis_index("row") % 2
-    ids = jnp.stack([place, low, place * 2 + low]).astype(jnp.int32)
+    keeps = lax.axis_index("row") // 2 % 2
+    ids = jnp.stack([place, low, place * 2 + low, keeps]).astype(jnp.int32)
 
     f32 = jnp.float32
     dma = pltpu.SemaphoreType.DMA
@@ -524,22 +614,30 @@
         1 << 31,
     )(pairing, ids, *parts)
     own_gram, cross_gram = sum_rows(own_grams, cross_grams)
+    own_gram, cross_gram = lax.optimization_barrier((own_gram, cross_gram))
+    cross_gram = cross_gram[:BLOCK] + exchange(cross_gram[BLOCK:], "row", 2)
 
     chain = 1 << 34
     (turned,) = call(
         first_round_kernel, [vmem], [(STEP_ROWS, order)], [pltpu.VMEM(square, f32)] + work_refs(), "first_round", chain
     )(own_gram)
     turned, cross_gram = lax.optimization_barrier((turned, cross_gram))
-    gathered, _ = gather_owners(turned, HALF_ROWS)
+    bit = 4
+    while bit < lax.axis_size("row"):
+        cross_gram = add_across(cross_gram, bit)
+        bit *= 2
+    gathered, (cross_gram, other_cross) = gather_owners(
+        turned, HALF_ROWS, cross_gram, lambda x: exchange(x, "row", 2)
+    )
     turned_parts, layout = flat(gathered)
     (second,) = call(
         functools.partial(second_round_kernel, blocks, layout, total_rows),
-        [smem, smem] + [hbm] * len(turned_parts) + [vmem],
+        [smem, smem] + [hbm] * len(turned_parts) + [vmem, vmem],
         [(order + SUB, order)],
         [pltpu.VMEM((2, STEP_ROWS, order), f32), pltpu.VMEM(square, f32), dma((2,))] + work_refs(),
         "second_round",
         chain,
-    )(pairing, ids, *turned_parts, cross_gram)
+    )(pairing, ids, *turned_parts, cross_gram, other_cross)
     parts, second = lax.optimization_barrier((parts, second))
     (columns,) = call(
         functools.partial(first_turn_kernel, slots, places, layout),

time: 140 us -> 132 us (0.943)
  Pallas kernels: 53.4 us -> 47.3 us
  starting transfers between devices: 26.7 us -> 24.3 us
    pallas_call x1, Pallas kernels: 20.8 us -> 17.8 us  [shards(): call(functools.partial(second_round_kernel, blocks, layout, total_rows),...]
    pallas_call x1, Pallas kernels: 18.4 us -> 15.9 us  [shards(): call(first_round_kernel, [vmem], [(STEP_ROWS, order)], [pltpu.VMEM(square...]
    ppermute x27 -> x28, starting transfers between devices: 26.7 us -> 24.3 us  [exchange(): return lax.ppermute(x, axis, [(i, i ^ bit) for i in range(size)])]
    ppermute x27 -> x28, waiting for transfers between devices: 56.4 us -> 57.6 us  [exchange(): return lax.ppermute(x, axis, [(i, i ^ bit) for i in range(size)])]
  transfers between devices with their start and end apart: 27 -> 28, of which waited for: 17 -> 13; matrix products, arithmetic and copies ran while one was open for 0% -> 0% of each run, Pallas kernels for 19% -> 18%
where the time goes in v3:
time: 132 us
  waiting for transfers between devices  57.6 us (44%)
  Pallas kernels  47.3 us (36%)
  starting transfers between devices  24.3 us (18%)
  local copies, waits for them, and re-layouts  1.97 us (1%)
    ppermute x28, waiting for transfers between devices, exchange(): return lax.ppermute(x, axis, [(i, i ^ bit) for i in range(size)])  57.6 us
    ppermute x28, starting transfers between devices, exchange(): return lax.ppermute(x, axis, [(i, i ^ bit) for i in range(size)])  24.3 us
    pallas_call x1, Pallas kernels, shards(): call(functools.partial(second_round_kernel, blocks, layout, total_rows),...  17.8 us
    pallas_call x1, Pallas kernels, shards(): call(first_round_kernel, [vmem], [(STEP_ROWS, order)], [pltpu.VMEM(square...  15.9 us
    pallas_call x1, Pallas kernels, shards(): call(functools.partial(first_turn_kernel, slots, places, layout), [smem,...  4.7 us
    pallas_call x1, Pallas kernels, shards(): call(functools.partial(last_turn_kernel, slots, blocks, layout), [smem, s...  3.53 us
    pallas_call x1, Pallas kernels, shards(): call(functools.partial(cross_gram_kernel, slots, blocks), [smem, smem] +...  2.8 us
  transfers between devices with their start and end apart: 28, of which 13 were waited for; matrix products, arithmetic and copies ran while one was open for 0% of the time, Pallas kernels for 18%

profile of v3, /device:TPU:0, one launch (start us, length us, event | category | flops | bytes accessed | tf_op | source)
XLA Modules:
  0.0 132.4 jit_solution(9495754243719023580)
XLA Ops:
  0.6 3.0 %collective-permute-start.1 = (f32[512,512]{1,0:T(8,128)}, f32[512,512]{1,0:T(8,128)S(1)}, u32[]{:S(2)}, u32[]{:S(2)}) collective-permute-start(f32[512,512]{1,0:T(8,128)} %refs_0_.4), channel_id=1, source_target_pairs={{0,2},{1,3},{2,0},{3,1},{4,6},{5,7},{6,4},{7,5},{8,10},{9,11},{10,... | collective-permute-start | bytes 3145736 | tf_op jit(solution)/shard_map/ppermute | solution.py:504
  3.7 23.4 %collective-permute-done.1.refs_2_ = f32[512,512]{1,0:T(8,128)S(1)} collective-permute-done((f32[512,512]{1,0:T(8,128)}, f32[512,512]{1,0:T(8,128)S(1)}, u32[]{:S(2)}, u32[]{:S(2)}) %collective-permute-start.1) | collective-permute-done | bytes 1048608 | tf_op jit(solution)/shard_map/ppermute | solution.py:504
  27.1 2.6 %collective-permute-done.2.refs_3_ = f32[512,512]{1,0:T(8,128)S(1)} collective-permute-done((f32[512,512]{1,0:T(8,128)S(1)}, f32[512,512]{1,0:T(8,128)S(1)}, u32[]{:S(2)}, u32[]{:S(2)}) %collective-permute-start.2) | collective-permute-done | bytes 1048608 | tf_op jit(solution)/shard_map/ppermute | solution.py:504
  31.6 2.5 %own_gram.1 = (f32[264,128]{1,0:T(8,128)S(1)}, f32[264,128]{1,0:T(8,128)S(1)}) custom-call(s32[2,16]{1,0:T(2,128)S(1)} %copy-done.2, s32[4]{0:T(128)S(1)} %pad_add_fusion.ids, f32[512,512]{1,0:T(8,128)S(1)} %copy-done, f32[512,512]{1,0:T(8,128)S(1)} %collective-permute-done.refs_1_, f32[512,512]{1,0:T(8,128)S(1)} %collective-permute-done.1.refs_2_, ...), custom_call_target="tpu_custom_call" | custom-call | bytes 1048576 | tf_op jit(solution)/shard_map/own_gram/pallas_call | solution.py:601
  34.2 1.8 %collective-permute-start.3 = (f32[264,128]{1,0:T(8,128)S(1)}, f32[264,128]{1,0:T(8,128)S(1)}, u32[]{:S(2)}, u32[]{:S(2)}) collective-permute-start(f32[264,128]{1,0:T(8,128)S(1)} %get-tuple-element.35), channel_id=1, source_target_pairs={{0,4},{4,0},{8,12},{12,8},{16,20},{20,16},{24,28},{28,24},{1,5},{5... | collective-permute-start | bytes 405512 | tf_op jit(solution)/shard_map/ppermute | solution.py:504
  35.9 3.9 %collective-permute-done.3 = f32[264,128]{1,0:T(8,128)S(1)} collective-permute-done((f32[264,128]{1,0:T(8,128)S(1)}, f32[264,128]{1,0:T(8,128)S(1)}, u32[]{:S(2)}, u32[]{:S(2)}) %collective-permute-start.3) | collective-permute-done | bytes 135200 | tf_op jit(solution)/shard_map/ppermute | solution.py:504
  39.9 1.9 %collective-permute-start.4 = (f32[264,128]{1,0:T(8,128)S(1)}, f32[264,128]{1,0:T(8,128)S(1)}, u32[]{:S(2)}, u32[]{:S(2)}) collective-permute-start(f32[264,128]{1,0:T(8,128)S(1)} %add.32), channel_id=1, source_target_pairs={{0,8},{4,12},{8,0},{12,4},{16,24},{20,28},{24,16},{28,20},{1,9},{5... | collective-permute-start | bytes 405512 | tf_op jit(solution)/shard_map/ppermute | solution.py:504
  41.7 2.8 %cross_gram.1 = (f32[256,256]{1,0:T(8,128)S(1)}, f32[256,256]{1,0:T(8,128)S(1)}) custom-call(s32[2,16]{1,0:T(2,128)S(1)} %copy-done.2, s32[4]{0:T(128)S(1)} %pad_add_fusion.ids, f32[512,512]{1,0:T(8,128)S(1)} %copy-done, f32[512,512]{1,0:T(8,128)S(1)} %collective-permute-done.refs_1_, f32[512,512]{1,0:T(8,128)S(1)} %collective-permute-done.1.refs_2_, ...), custom_call_target="tpu_custom_call" | custom-call | flops 2147483648 | bytes 1048576 | tf_op jit(solution)/shard_map/cross_gram/pallas_call | solution.py:608
  45.0 1.8 %collective-permute-start.6 = (f32[256,256]{1,0:T(8,128)S(1)}, f32[256,256]{1,0:T(8,128)S(1)}, u32[]{:S(2)}, u32[]{:S(2)}) collective-permute-start(f32[256,256]{1,0:T(8,128)S(1)} %get-tuple-element.40), channel_id=1, source_target_pairs={{0,4},{4,0},{8,12},{12,8},{16,20},{20,16},{24,28},{28,24},{1,5},{5... | collective-permute-start | bytes 786440 | tf_op jit(solution)/shard_map/ppermute | solution.py:504
  46.7 2.6 %collective-permute-start.5 = (f32[264,128]{1,0:T(8,128)S(1)}, f32[264,128]{1,0:T(8,128)S(1)}, u32[]{:S(2)}, u32[]{:S(2)}) collective-permute-start(f32[264,128]{1,0:T(8,128)S(1)} %add.33), channel_id=1, source_target_pairs={{0,16},{4,20},{8,24},{12,28},{16,0},{20,4},{24,8},{28,12},{1,17},{... | collective-permute-start | bytes 405512 | tf_op jit(solution)/shard_map/ppermute | solution.py:504
  49.3 4.9 %collective-permute-done.5 = f32[264,128]{1,0:T(8,128)S(1)} collective-permute-done((f32[264,128]{1,0:T(8,128)S(1)}, f32[264,128]{1,0:T(8,128)S(1)}, u32[]{:S(2)}, u32[]{:S(2)}) %collective-permute-start.5) | collective-permute-done | bytes 135200 | tf_op jit(solution)/shard_map/ppermute | solution.py:504
  54.9 15.9 %first_round.1.refs_0_.refs_4_ = f32[328,256]{1,0:T(8,128)S(1)} custom-call(f32[264,128]{1,0:T(8,128)S(1)} %add.34.parts_ref), custom_call_target="tpu_custom_call" | custom-call | flops 17179869184 | bytes 1048576 | tf_op jit(solution)/shard_map/first_round/pallas_call | solution.py:621
  71.0 1.6 %collective-permute-start.9 = (f32[328,256]{1,0:T(8,128)S(1)}, f32[328,256]{1,0:T(8,128)S(1)}, u32[]{:S(2)}, u32[]{:S(2)}) collective-permute-start(f32[328,256]{1,0:T(8,128)S(1)} %first_round.1.refs_0_.refs_4_), channel_id=1, source_target_pairs={{0,2},{1,3},{2,0},{3,1},{4,6},{5,7},{6,4},{7,5},{8,10},{9,11},{10,... | collective-permute-start | bytes 1007624 | tf_op jit(solution)/shard_map/ppermute | solution.py:504
  73.1 3.4 %collective-permute-start.11 = (f32[128,256]{1,0:T(8,128)S(1)}, f32[128,256]{1,0:T(8,128)S(1)}, u32[]{:S(2)}, u32[]{:S(2)}) collective-permute-start(f32[128,256]{1,0:T(8,128)S(1)} %slice_add_fusion), channel_id=1, source_target_pairs={{0,16},{4,20},{8,24},{12,28},{16,0},{20,4},{24,8},{28,12},{1,17},{... | collective-permute-start | bytes 393224 | tf_op jit(solution)/shard_map/ppermute | solution.py:504
  76.5 6.4 %collective-permute-done.11 = f32[128,256]{1,0:T(8,128)S(1)} collective-permute-done((f32[128,256]{1,0:T(8,128)S(1)}, f32[128,256]{1,0:T(8,128)S(1)}, u32[]{:S(2)}, u32[]{:S(2)}) %collective-permute-start.11) | collective-permute-done | bytes 131104 | tf_op jit(solution)/shard_map/ppermute | solution.py:504
  83.0 1.6 %collective-permute-start.14 = (f32[168,256]{1,0:T(8,128)S(1)}, f32[168,256]{1,0:T(8,128)S(1)}, u32[]{:S(2)}, u32[]{:S(2)}) collective-permute-start(f32[168,256]{1,0:T(8,128)S(1)} %slice.21), channel_id=1, source_target_pairs={{0,4},{4,0},{8,12},{12,8},{16,20},{20,16},{24,28},{28,24},{1,5},{5... | collective-permute-start | bytes 516104 | tf_op jit(solution)/shard_map/ppermute | solution.py:504
  85.7 5.4 %collective-permute-done.15.refs_11_ = f32[128,256]{1,0:T(8,128)S(1)} collective-permute-done((f32[128,256]{1,0:T(8,128)S(1)}, f32[128,256]{1,0:T(8,128)S(1)}, u32[]{:S(2)}, u32[]{:S(2)}) %collective-permute-start.15) | collective-permute-done | bytes 131104 | tf_op jit(solution)/shard_map/ppermute | solution.py:504
  92.7 17.8 %second_round.1.refs_0_ = f32[264,256]{1,0:T(8,128)S(1)} custom-call(s32[2,16]{1,0:T(2,128)S(1)} %copy-done.3, s32[4]{0:T(128)S(1)} %pad_add_fusion.ids, f32[328,256]{1,0:T(8,128)S(1)} %first_round.1.refs_0_.refs_4_, f32[328,256]{1,0:T(8,128)S(1)} %collective-permute-done.8.refs_1_.refs_5_, f32[328,256]{1,0:T(8,128)S(1)} %collective-permute-done.10.refs_2_.refs_6_, ...), custom_call_target="tpu_custom_call" | custom-call | flops 17179869184 | bytes 1048576 | tf_op jit(solution)/shard_map/second_round/pallas_call | solution.py:633
  110.6 1.8 %collective-permute-start.20 = (f32[264,256]{1,0:T(8,128)S(1)}, f32[264,256]{1,0:T(8,128)S(1)}, u32[]{:S(2)}, u32[]{:S(2)}) collective-permute-start(f32[264,256]{1,0:T(8,128)S(1)} %second_round.1.refs_0_), channel_id=1, source_target_pairs={{0,2},{1,3},{2,0},{3,1},{4,6},{5,7},{6,4},{7,5},{8,10},{9,11},{10,... | collective-permute-start | bytes 811016 | tf_op jit(solution)/shard_map/ppermute | solution.py:504
  112.7 4.7 %first_turn.1.columns_ref = f32[4,512,256]{2,1,0:T(8,128)S(1)} custom-call(s32[2,16]{1,0:T(2,128)S(1)} %copy-done.3, s32[4]{0:T(128)S(1)} %pad_add_fusion.ids, f32[512,512]{1,0:T(8,128)S(1)} %copy-done.1, f32[512,512]{1,0:T(8,128)S(1)} %collective-permute-done.refs_1_, f32[512,512]{1,0:T(8,128)S(1)} %collective-permute-done.1.refs_2_, ...), custom_call_target="tpu_custom_call" | custom-call | flops 4294967296 | bytes 1048576 | tf_op jit(solution)/shard_map/first_turn/pallas_call | solution.py:642
  117.4 2.1 %collective-permute-done.20.refs_4_ = f32[264,256]{1,0:T(8,128)S(1)} collective-permute-done((f32[264,256]{1,0:T(8,128)S(1)}, f32[264,256]{1,0:T(8,128)S(1)}, u32[]{:S(2)}, u32[]{:S(2)}) %collective-permute-start.20) | collective-permute-done | bytes 270368 | tf_op jit(solution)/shard_map/ppermute | solution.py:504
  122.2 3.4 %collective-permute-done.24.refs_6_ = f32[136,256]{1,0:T(8,128)S(1)} collective-permute-done((f32[136,256]{1,0:T(8,128)S(1)}, f32[136,256]{1,0:T(8,128)S(1)}, u32[]{:S(2)}, u32[]{:S(2)}) %collective-permute-start.24) | collective-permute-done | bytes 139296 | tf_op jit(solution)/shard_map/ppermute | solution.py:504
  125.7 1.7 %collective-permute-done.23.refs_5_ = f32[128,256]{1,0:T(8,128)S(1)} collective-permute-done((f32[128,256]{1,0:T(8,128)S(1)}, f32[128,256]{1,0:T(8,128)S(1)}, u32[]{:S(2)}, u32[]{:S(2)}) %collective-permute-start.23) | collective-permute-done | bytes 131104 | tf_op jit(solution)/shard_map/ppermute | solution.py:504
  128.7 3.5 %last_turn.1 = (f32[512,512]{1,0:T(8,128)}, f32[1,512]{1,0:T(1,128)}) custom-call(s32[2,16]{1,0:T(2,128)S(1)} %copy-done.3, s32[4]{0:T(128)S(1)} %pad_add_fusion.ids, f32[4,512,256]{2,1,0:T(8,128)S(1)} %first_turn.1.columns_ref, f32[264,256]{1,0:T(8,128)S(1)} %second_round.1.refs_0_, f32[264,256]{1,0:T(8,128)S(1)} %collective-permute-done.19.refs_1_, ...), custom_call_target="tpu_custom_call" | custom-call | bytes 1048576 | tf_op jit(solution)/shard_map/last_turn/pallas_call | solution.py:656
  (58 shorter events, 11.1 us)
Async XLA Ops:
  0.6 26.4 %collective-permute-start.1 = (f32[512,512]{1,0:T(8,128)}, f32[512,512]{1,0:T(8,128)S(1)}, u32[]{:S(2)}, u32[]{:S(2)}) collective-permute-start(f32[512,512]{1,0:T(8,128)} %refs_0_.4), channel_id=1, source_target_pairs={{0,2},{1,3},{2,0},{3,1},{4,6},{5,7},{6,4},{7,5},{8,10},{9,11},{10,... | collective-permute-start | bytes 3145736 | tf_op jit(solution)/shard_map/ppermute | solution.py:504
  3.7 23.5 %collective-permute-start = (f32[512,512]{1,0:T(8,128)}, f32[512,512]{1,0:T(8,128)S(1)}, u32[]{:S(2)}, u32[]{:S(2)}) collective-permute-start(f32[512,512]{1,0:T(8,128)} %refs_0_.4), channel_id=1, source_target_pairs={{0,1},{1,0},{2,3},{3,2},{4,5},{5,4},{6,7},{7,6},{8,9},{9,8},{10,11... | collective-permute-start | bytes 3145736 | tf_op jit(solution)/shard_map/ppermute | solution.py:504
  34.2 5.7 %collective-permute-start.3 = (f32[264,128]{1,0:T(8,128)S(1)}, f32[264,128]{1,0:T(8,128)S(1)}, u32[]{:S(2)}, u32[]{:S(2)}) collective-permute-start(f32[264,128]{1,0:T(8,128)S(1)} %get-tuple-element.35), channel_id=1, source_target_pairs={{0,4},{4,0},{8,12},{12,8},{16,20},{20,16},{24,28},{28,24},{1,5},{5... | collective-permute-start | bytes 405512 | tf_op jit(solution)/shard_map/ppermute | solution.py:504
  39.9 5.1 %collective-permute-start.4 = (f32[264,128]{1,0:T(8,128)S(1)}, f32[264,128]{1,0:T(8,128)S(1)}, u32[]{:S(2)}, u32[]{:S(2)}) collective-permute-start(f32[264,128]{1,0:T(8,128)S(1)} %add.32), channel_id=1, source_target_pairs={{0,8},{4,12},{8,0},{12,4},{16,24},{20,28},{24,16},{28,20},{1,9},{5... | collective-permute-start | bytes 405512 | tf_op jit(solution)/shard_map/ppermute | solution.py:504
  45.0 9.2 %collective-permute-start.6 = (f32[256,256]{1,0:T(8,128)S(1)}, f32[256,256]{1,0:T(8,128)S(1)}, u32[]{:S(2)}, u32[]{:S(2)}) collective-permute-start(f32[256,256]{1,0:T(8,128)S(1)} %get-tuple-element.40), channel_id=1, source_target_pairs={{0,4},{4,0},{8,12},{12,8},{16,20},{20,16},{24,28},{28,24},{1,5},{5... | collective-permute-start | bytes 786440 | tf_op jit(solution)/shard_map/ppermute | solution.py:504
  46.7 7.4 %collective-permute-start.5 = (f32[264,128]{1,0:T(8,128)S(1)}, f32[264,128]{1,0:T(8,128)S(1)}, u32[]{:S(2)}, u32[]{:S(2)}) collective-permute-start(f32[264,128]{1,0:T(8,128)S(1)} %add.33), channel_id=1, source_target_pairs={{0,16},{4,20},{8,24},{12,28},{16,0},{20,4},{24,8},{28,12},{1,17},{... | collective-permute-start | bytes 405512 | tf_op jit(solution)/shard_map/ppermute | solution.py:504
  54.3 16.6 %collective-permute-start.7 = (f32[128,256]{1,0:T(8,128)S(1)}, f32[128,256]{1,0:T(8,128)S(1)}, u32[]{:S(2)}, u32[]{:S(2)}) collective-permute-start(f32[128,256]{1,0:T(8,128)S(1)} %slice.19), channel_id=1, source_target_pairs={{0,8},{4,12},{8,0},{12,4},{16,24},{20,28},{24,16},{28,20},{1,9},{5... | collective-permute-start | bytes 393224 | tf_op jit(solution)/shard_map/ppermute | solution.py:504
  70.9 12.0 %collective-permute-start.10 = (f32[328,256]{1,0:T(8,128)S(1)}, f32[328,256]{1,0:T(8,128)S(1)}, u32[]{:S(2)}, u32[]{:S(2)}) collective-permute-start(f32[328,256]{1,0:T(8,128)S(1)} %first_round.1.refs_0_.refs_4_), channel_id=1, source_target_pairs={{0,1},{1,0},{2,3},{3,2},{4,5},{5,4},{6,7},{7,6},{8,9},{9,8},{10,11... | collective-permute-start | bytes 1007624 | tf_op jit(solution)/shard_map/ppermute | solution.py:504
  71.0 11.9 %collective-permute-start.9 = (f32[328,256]{1,0:T(8,128)S(1)}, f32[328,256]{1,0:T(8,128)S(1)}, u32[]{:S(2)}, u32[]{:S(2)}) collective-permute-start(f32[328,256]{1,0:T(8,128)S(1)} %first_round.1.refs_0_.refs_4_), channel_id=1, source_target_pairs={{0,2},{1,3},{2,0},{3,1},{4,6},{5,7},{6,4},{7,5},{8,10},{9,11},{10,... | collective-permute-start | bytes 1007624 | tf_op jit(solution)/shard_map/ppermute | solution.py:504
  72.6 10.4 %collective-permute-start.8 = (f32[328,256]{1,0:T(8,128)S(1)}, f32[328,256]{1,0:T(8,128)S(1)}, u32[]{:S(2)}, u32[]{:S(2)}) collective-permute-start(f32[328,256]{1,0:T(8,128)S(1)} %first_round.1.refs_0_.refs_4_), channel_id=1, source_target_pairs={{0,4},{4,0},{8,12},{12,8},{16,20},{20,16},{24,28},{28,24},{1,5},{5... | collective-permute-start | bytes 1007624 | tf_op jit(solution)/shard_map/ppermute | solution.py:504
  73.1 9.8 %collective-permute-start.11 = (f32[128,256]{1,0:T(8,128)S(1)}, f32[128,256]{1,0:T(8,128)S(1)}, u32[]{:S(2)}, u32[]{:S(2)}) collective-permute-start(f32[128,256]{1,0:T(8,128)S(1)} %slice_add_fusion), channel_id=1, source_target_pairs={{0,16},{4,20},{8,24},{12,28},{16,0},{20,4},{24,8},{28,12},{1,17},{... | collective-permute-start | bytes 393224 | tf_op jit(solution)/shard_map/ppermute | solution.py:504
  83.0 8.1 %collective-permute-start.14 = (f32[168,256]{1,0:T(8,128)S(1)}, f32[168,256]{1,0:T(8,128)S(1)}, u32[]{:S(2)}, u32[]{:S(2)}) collective-permute-start(f32[168,256]{1,0:T(8,128)S(1)} %slice.21), channel_id=1, source_target_pairs={{0,4},{4,0},{8,12},{12,8},{16,20},{20,16},{24,28},{28,24},{1,5},{5... | collective-permute-start | bytes 516104 | tf_op jit(solution)/shard_map/ppermute | solution.py:504
  84.5 6.5 %collective-permute-start.13 = (f32[160,256]{1,0:T(8,128)S(1)}, f32[160,256]{1,0:T(8,128)S(1)}, u32[]{:S(2)}, u32[]{:S(2)}) collective-permute-start(f32[160,256]{1,0:T(8,128)S(1)} %slice.20), channel_id=1, source_target_pairs={{0,2},{1,3},{2,0},{3,1},{4,6},{5,7},{6,4},{7,5},{8,10},{9,11},{10,... | collective-permute-start | bytes 491528 | tf_op jit(solution)/shard_map/ppermute | solution.py:504
  85.1 7.6 %collective-permute-start.12 = (f32[328,256]{1,0:T(8,128)S(1)}, f32[328,256]{1,0:T(8,128)S(1)}, u32[]{:S(2)}, u32[]{:S(2)}) collective-permute-start(f32[328,256]{1,0:T(8,128)S(1)} %collective-permute-done.8.refs_1_.refs_5_), channel_id=1, source_target_pairs={{0,1},{1,0},{2,3},{3,2},{4,5},{5,4},{6,7},{7,6},{8,9},{9,8},{10,11... | collective-permute-start | bytes 1007624 | tf_op jit(solution)/shard_map/ppermute | solution.py:504
  85.1 7.6 %collective-permute-start.16 = (f32[328,256]{1,0:T(8,128)S(1)}, f32[328,256]{1,0:T(8,128)S(1)}, u32[]{:S(2)}, u32[]{:S(2)}) collective-permute-start(f32[328,256]{1,0:T(8,128)S(1)} %collective-permute-done.9.refs_4_.refs_8_), channel_id=1, source_target_pairs={{0,1},{1,0},{2,3},{3,2},{4,5},{5,4},{6,7},{7,6},{8,9},{9,8},{10,11... | collective-permute-start | bytes 1007624 | tf_op jit(solution)/shard_map/ppermute | solution.py:504
  85.6 5.4 %collective-permute-start.15 = (f32[128,256]{1,0:T(8,128)S(1)}, f32[128,256]{1,0:T(8,128)S(1)}, u32[]{:S(2)}, u32[]{:S(2)}) collective-permute-start(f32[128,256]{1,0:T(8,128)S(1)} %add.37.refs_10_), channel_id=1, source_target_pairs={{0,8},{4,12},{8,0},{12,4},{16,24},{20,28},{24,16},{28,20},{1,9},{5... | collective-permute-start | bytes 393224 | tf_op jit(solution)/shard_map/ppermute | solution.py:504
  110.5 6.9 %collective-permute-start.21 = (f32[264,256]{1,0:T(8,128)S(1)}, f32[264,256]{1,0:T(8,128)S(1)}, u32[]{:S(2)}, u32[]{:S(2)}) collective-permute-start(f32[264,256]{1,0:T(8,128)S(1)} %second_round.1.refs_0_), channel_id=1, source_target_pairs={{0,1},{1,0},{2,3},{3,2},{4,5},{5,4},{6,7},{7,6},{8,9},{9,8},{10,11... | collective-permute-start | bytes 811016 | tf_op jit(solution)/shard_map/ppermute | solution.py:504
  110.6 8.9 %collective-permute-start.20 = (f32[264,256]{1,0:T(8,128)S(1)}, f32[264,256]{1,0:T(8,128)S(1)}, u32[]{:S(2)}, u32[]{:S(2)}) collective-permute-start(f32[264,256]{1,0:T(8,128)S(1)} %second_round.1.refs_0_), channel_id=1, source_target_pairs={{0,2},{1,3},{2,0},{3,1},{4,6},{5,7},{6,4},{7,5},{8,10},{9,11},{10,... | collective-permute-start | bytes 811016 | tf_op jit(solution)/shard_map/ppermute | solution.py:504
  112.4 8.2 %collective-permute-start.19 = (f32[264,256]{1,0:T(8,128)S(1)}, f32[264,256]{1,0:T(8,128)S(1)}, u32[]{:S(2)}, u32[]{:S(2)}) collective-permute-start(f32[264,256]{1,0:T(8,128)S(1)} %second_round.1.refs_0_), channel_id=1, source_target_pairs={{0,4},{4,0},{8,12},{12,8},{16,20},{20,16},{24,28},{28,24},{1,5},{5... | collective-permute-start | bytes 811016 | tf_op jit(solution)/shard_map/ppermute | solution.py:504
  120.6 5.1 %collective-permute-start.24 = (f32[136,256]{1,0:T(8,128)S(1)}, f32[136,256]{1,0:T(8,128)S(1)}, u32[]{:S(2)}, u32[]{:S(2)}) collective-permute-start(f32[136,256]{1,0:T(8,128)S(1)} %slice.23), channel_id=1, source_target_pairs={{0,4},{4,0},{8,12},{12,8},{16,20},{20,16},{24,28},{28,24},{1,5},{5... | collective-permute-start | bytes 417800 | tf_op jit(solution)/shard_map/ppermute | solution.py:504
  121.4 7.3 %collective-permute-start.22 = (f32[264,256]{1,0:T(8,128)S(1)}, f32[264,256]{1,0:T(8,128)S(1)}, u32[]{:S(2)}, u32[]{:S(2)}) collective-permute-start(f32[264,256]{1,0:T(8,128)S(1)} %collective-permute-done.19.refs_1_), channel_id=1, source_target_pairs={{0,1},{1,0},{2,3},{3,2},{4,5},{5,4},{6,7},{7,6},{8,9},{9,8},{10,11... | collective-permute-start | bytes 811016 | tf_op jit(solution)/shard_map/ppermute | solution.py:504
  121.4 7.3 %collective-permute-start.25 = (f32[264,256]{1,0:T(8,128)S(1)}, f32[264,256]{1,0:T(8,128)S(1)}, u32[]{:S(2)}, u32[]{:S(2)}) collective-permute-start(f32[264,256]{1,0:T(8,128)S(1)} %collective-permute-done.20.refs_4_), channel_id=1, source_target_pairs={{0,1},{1,0},{2,3},{3,2},{4,5},{5,4},{6,7},{7,6},{8,9},{9,8},{10,11... | collective-permute-start | bytes 811016 | tf_op jit(solution)/shard_map/ppermute | solution.py:504
  121.9 5.5 %collective-permute-start.23 = (f32[128,256]{1,0:T(8,128)S(1)}, f32[128,256]{1,0:T(8,128)S(1)}, u32[]{:S(2)}, u32[]{:S(2)}) collective-permute-start(f32[128,256]{1,0:T(8,128)S(1)} %slice.22), channel_id=1, source_target_pairs={{0,2},{1,3},{2,0},{3,1},{4,6},{5,7},{6,4},{7,5},{8,10},{9,11},{10,... | collective-permute-start | bytes 393224 | tf_op jit(solution)/shard_map/ppermute | solution.py:504
  125.7 3.0 %collective-permute-start.27 = (f32[136,256]{1,0:T(8,128)S(1)}, f32[136,256]{1,0:T(8,128)S(1)}, u32[]{:S(2)}, u32[]{:S(2)}) collective-permute-start(f32[136,256]{1,0:T(8,128)S(1)} %collective-permute-done.24.refs_6_), channel_id=1, source_target_pairs={{0,1},{1,0},{2,3},{3,2},{4,5},{5,4},{6,7},{7,6},{8,9},{9,8},{10,11... | collective-permute-start | bytes 417800 | tf_op jit(solution)/shard_map/ppermute | solution.py:504
  (8 other events, 75.8 us)
